TPU v7x, 512 devices: a whole 4x8x8 slice. The times are simulated.
512 devices in a mesh: tile: 64 (over x, z, core), lev: 8 (over y).
Axes of the slice: x: 4, y: 8, z: 8, core: 2. Of those that a mesh axis runs over, the one named last changes fastest.
Arguments:
- grid_state: bfloat16 [8, 8192, 512], P('lev', 'tile'), may hold values from -28 to 28
- observations: bfloat16 [32768, 256], P('tile'), may hold values from -28 to 28
- destination: int32 [32768, 1], P('tile'), may hold values from 0 to 63; in each aligned block of 512 rows (0 to 511, 512 to 1023, ...) at most 16 rows name the same one
- subtile: int32 [32768], P('tile'), may hold values from 0 to 3
- query_weight: bfloat16 [512, 512], replicated, may hold values from -0.25 to 0.25
- key_weight: bfloat16 [256, 512], replicated, may hold values from -0.375 to 0.375
- value_weight: bfloat16 [256, 512], replicated, may hold values from -0.375 to 0.375
- out_weight: bfloat16 [512, 512], replicated, may hold values from -0.25 to 0.25
- sink_logit: float32 [8], replicated, may hold values from 0 to 4
- norm_gain: float32 [512], replicated, may hold values from 0.1 to 1.9
- mixing: float32 [8, 8], replicated, may hold values from -2 to 2
- up_weight: bfloat16 [512, 1024], replicated, may hold values from -0.25 to 0.25
- down_weight: bfloat16 [1024, 512], replicated, may hold values from -0.1875 to 0.1875
Outputs:
- analysis: bfloat16 [8, 8192, 512], P('lev', 'tile')
Inputs may be any that keep to these rules, and one draw needn't show every extreme that they name: `destination`: at most 16 of the tokens of one tile shard name one tile, a bound that some block reaches of them.
All inputs are finite; a program needn't handle non-finite values.
Results may differ from a plain program's by a relative error of at most 0.006.
The roundings to bfloat16 on the way count: a program that leaves them out, or rounds other values in their place, can miss the bound.
Values may be sent and summed in bfloat16 or wider, within the bound.
No kernel may reach another device: no remote copies, remote signals or barrier semaphores. Data moves between devices by JAX's collectives and lax.ppermute only.
A program may use at most 64 MiB of HBM per device.

v0:
```python
import math

import jax
import jax.numpy as jnp
from jax import lax
from jax.sharding import PartitionSpec as P

SUBCELLS = 32


def attend(queries, token_keys, token_values, valid, sink_logit):

    def per_head(operands):
        q_head, k_head, v_head, sink_head = operands
        scores = jnp.dot(q_head, k_head.T, preferred_element_type=jnp.float32) * (
            1.0 / math.sqrt(q_head.shape[1])
        )
        masked = jnp.where(valid, scores, -1e30)
        peak = jnp.maximum(jnp.max(masked, axis=1, keepdims=True), sink_head)
        weights = jnp.where(valid, jnp.exp(masked - peak), 0.0)
        denominator = jnp.exp(sink_head - peak) + jnp.sum(weights, axis=1, keepdims=True)
        probability = (weights / denominator).astype(jnp.bfloat16)
        return jnp.dot(probability, v_head, preferred_element_type=jnp.float32).astype(jnp.bfloat16)

    return lax.map(per_head, (queries, token_keys, token_values, sink_logit))


def split_heads(matrix, head_count):
    return matrix.reshape(matrix.shape[0], head_count, matrix.shape[1] // head_count).transpose(
        1, 0, 2
    )


def column_mlp(stacked, mix_rows, residual, norm_gain, up_weight, down_weight):
    wide = stacked.astype(jnp.float32)
    inverse = lax.rsqrt(jnp.mean(wide * wide, axis=2, keepdims=True) + 1e-05)
    normed = wide * inverse * norm_gain
    blended = jnp.einsum("lm,mcd->lcd", mix_rows, normed, precision=lax.Precision.HIGHEST).astype(
        jnp.bfloat16
    )
    hidden = jax.nn.gelu(jnp.dot(blended, up_weight, preferred_element_type=jnp.float32)).astype(
        jnp.bfloat16
    )
    return (
        residual.astype(jnp.float32)
        + jnp.dot(hidden, down_weight, preferred_element_type=jnp.float32)
    ).astype(jnp.bfloat16)


def body(
    grid_state,
    observations,
    destination,
    subtile,
    query_weight,
    key_weight,
    value_weight,
    out_weight,
    sink_logit,
    norm_gain,
    mixing,
    up_weight,
    down_weight,
):
    tile_count = lax.axis_size("tile")
    token_rows = observations.shape[0]
    capacity = 2 * token_rows // tile_count
    target = destination[:, 0]
    tile_ids = jnp.arange(tile_count, dtype=jnp.int32)
    onehot = (target[:, None] == tile_ids[None, :]).astype(jnp.int32)
    ranking = jnp.sum((jnp.cumsum(onehot, axis=0) - onehot) * onehot, axis=1)
    slot_index = target * capacity + ranking
    slot_codes = (
        jnp.zeros((tile_count * capacity,), jnp.bfloat16)
        .at[slot_index]
        .set((subtile + 1).astype(jnp.bfloat16))
    )
    slot_codes = slot_codes.reshape(tile_count, capacity)
    token_bank = (
        jnp.zeros((tile_count * capacity, observations.shape[1]), observations.dtype)
        .at[slot_index]
        .set(observations)
    )
    received = lax.all_to_all(
        token_bank.reshape(tile_count, capacity, observations.shape[1]),
        "tile",
        split_axis=0,
        concat_axis=0,
        tiled=True,
    )
    codes_in = lax.all_to_all(slot_codes, "tile", split_axis=0, concat_axis=0, tiled=True)
    slot_total = received.shape[0] * received.shape[1]
    tokens = received.reshape(slot_total, received.shape[2])
    codes_here = codes_in.reshape(slot_total).astype(jnp.int32)
    key_rows = jnp.dot(tokens, key_weight, preferred_element_type=jnp.float32).astype(jnp.bfloat16)
    value_rows = jnp.dot(tokens, value_weight, preferred_element_type=jnp.float32).astype(
        jnp.bfloat16
    )
    level_here = grid_state.shape[0]
    cells_here = grid_state.shape[1]
    width_grid = grid_state.shape[2]
    grid_rows = grid_state.reshape(level_here * cells_here, width_grid)
    queries = jnp.dot(grid_rows, query_weight, preferred_element_type=jnp.float32).astype(
        jnp.bfloat16
    )
    cell_sub = jnp.tile(jnp.arange(cells_here, dtype=jnp.int32) // SUBCELLS, level_here)
    valid = (codes_here[None, :] > 0) & (jnp.abs(codes_here[None, :] - 1 - cell_sub[:, None]) <= 1)
    head_count = sink_logit.shape[0]
    head_out = attend(
        split_heads(queries, head_count),
        split_heads(key_rows, head_count),
        split_heads(value_rows, head_count),
        valid,
        sink_logit,
    )
    attended = head_out.transpose(1, 0, 2).reshape(grid_rows.shape[0], width_grid)
    updated = (
        grid_rows.astype(jnp.float32)
        + jnp.dot(attended, out_weight, preferred_element_type=jnp.float32)
    ).astype(jnp.bfloat16)
    updated = updated.reshape(level_here, cells_here, width_grid)
    columns = lax.all_to_all(updated, "lev", split_axis=1, concat_axis=0, tiled=True)
    encoded = column_mlp(columns, mixing, columns, norm_gain, up_weight, down_weight)
    analysis = lax.all_to_all(encoded, "lev", split_axis=0, concat_axis=1, tiled=True)
    return analysis


def solution(mesh):
    placed = (
        P("lev", "tile", None),
        P("tile", None),
        P("tile", None),
        P("tile"),
        P(),
        P(),
        P(),
        P(),
        P(),
        P(),
        P(),
        P(),
        P(),
    )
    return jax.shard_map(
        body, mesh=mesh, in_specs=placed, out_specs=P("lev", "tile", None), check_vma=False
    )
```

profile of v0, /device:TPU:6, one launch (start us, length us, event | category | flops | bytes accessed | tf_op | source)
XLA Modules:
  0.0 132.9 jit_solution(6042436196607123952)
XLA Ops:
  0.0 0.8 fusion.52
  0.9 1.2 reduce-window.6
  2.3 0.8 fusion.48
  3.1 0.7 compare_select_fusion
  3.8 0.7 add_convert_fusion
  4.5 3.8 %scatter_custom_fusion.1 = bf16[1024]{0:T(1024)(128)(2,1)S(1)} fusion(s32[512]{0:T(512)S(1)} %bitcast.117, bf16[512]{0:T(512)(128)(2,1)S(1)} %add_convert_fusion, bf16[]{:T(256)} %constant.30.clone.1), kind=kCustom, calls=%fused_computation.76 | custom fusion | bytes 2050 | tf_op jit(solution)/shard_map/scatter | solution.py:76
  8.3 0.7 all_to_all.31
  9.0 14.0 %all-to-all-start.1 = ((bf16[64,1,16]{2,1,0:T(2,128)(2,1)}), bf16[64,1,16]{2,1,0:T(2,128)(2,1)S(1)}, u32[]{:S(2)}, u32[]{:S(2)}) async-start(bf16[64,1,16]{2,1,0:T(2,128)(2,1)} %all_to_all.31), calls=%async_computation.1 | async-start | bytes 65536 | tf_op jit(solution)/shard_map/all_to_all | solution.py:91
  23.0 3.5 %scatter_custom_fusion = bf16[1024,256]{1,0:T(8,128)(2,1)} fusion(s32[512]{0:T(512)S(1)} %bitcast.118, bf16[512,256]{1,0:T(8,128)(2,1)} %param.16, bf16[]{:T(256)} %constant.30.clone.1), kind=kCustom, calls=%fused_computation.54 | custom fusion | bytes 524800 | tf_op jit(solution)/shard_map/scatter | solution.py:82
  26.5 4.0 %all-to-all-done.1 = bf16[64,1,16]{2,1,0:T(2,128)(2,1)S(1)} async-done(((bf16[64,1,16]{2,1,0:T(2,128)(2,1)}), bf16[64,1,16]{2,1,0:T(2,128)(2,1)S(1)}, u32[]{:S(2)}, u32[]{:S(2)}) %all-to-all-start.1) | async-done | bytes 2080 | tf_op jit(solution)/shard_map/all_to_all | solution.py:91
  30.5 6.6 %all-to-all-start = ((bf16[64,16,256]{2,1,0:T(8,128)(2,1)}), bf16[64,16,256]{2,1,0:T(8,128)(2,1)S(1)}, u32[]{:S(2)}, u32[]{:S(2)}) async-start(bf16[64,16,256]{2,1,0:T(8,128)(2,1)} %bitcast.8), calls=%async_computation | async-start | bytes 1048576 | tf_op jit(solution)/shard_map/all_to_all | solution.py:84
  37.9 15.9 %all-to-all-done = bf16[64,16,256]{2,1,0:T(8,128)(2,1)S(1)} async-done(((bf16[64,16,256]{2,1,0:T(8,128)(2,1)}), bf16[64,16,256]{2,1,0:T(8,128)(2,1)S(1)}, u32[]{:S(2)}, u32[]{:S(2)}) %all-to-all-start) | async-done | bytes 524320 | tf_op jit(solution)/shard_map/all_to_all | solution.py:84
  54.3 1.8 %copy.24 = bf16[1024,8,64]{2,0,1:T(8,128)(2,1)} copy(bf16[1024,8,64]{0,2,1:T(8,128)(2,1)S(1)} %bitcast.104) | data formatting | bytes 2097152 | tf_op jit(solution)/shard_map/reshape | solution.py:29
  56.6 1.8 %copy.25 = bf16[1024,8,64]{2,0,1:T(8,128)(2,1)} copy(bf16[1024,8,64]{0,2,1:T(8,128)(2,1)S(1)} %bitcast.103) | data formatting | bytes 2097152 | tf_op jit(solution)/shard_map/reshape | solution.py:29
  58.4 40.6 %while.11 = (s32[]{:T(128)}, bf16[8,128,64]{1,2,0:T(8,128)(2,1)S(1)}, bf16[8,128,64]{1,2,0:T(8,128)(2,1)S(1)}, bf16[8,1024,64]{2,1,0:T(8,128)(2,1)}, f32[8]{0:T(...) while((s32[]{:T(128)}, ...), condition=%wide.region_8.9_spmd.clone, body=%wide.region_5.8_spmd.clone.sunk | while | flops 36446464 | bytes 2154105 | solution.py:25
  58.4 1.4 %fusion.73 = (f32[128]{0:T(128)S(1)}, f32[128,1024]{1,0:T(8,128)S(1)}) fusion(bf16[8,1024,64]{2,1,0:T(8,128)(2,1)} %get-tuple-element.186, s32[]{:T(128)} %get-tuple-element.173, bf16[8,128,64]{1,2,0:T(8,128)(2,1)S(1)} %get-tuple-element.185, s32[128]{0:T(128)S(1)} %get-tuple-element.189, s32[1024]{0:T(1024)S(1)} %get-tuple-element.190, ...), kind=kOutput, calls=%fused_computation.83.clone.1 | convolution fusion | flops 17694592 | bytes 809984 | tf_op jit(solution)/shard_map/while/body/eval_jaxpr/dot_general | solution.py:15
  60.4 0.6 broadcast_maximum_fusion.2
  61.4 0.7 exponential_add_fusion.2
  62.1 1.4 %fusion.75 = bf16[8,128,64]{1,2,0:T(8,128)(2,1)S(1)} fusion(bf16[8,128,64]{1,2,0:T(8,128)(2,1)S(1)} %get-tuple-element.174, s32[]{:T(128)} %get-tuple-element.173, bf16[8,1024,64]{2,1,0:T(8,128)(2,1)} %get-tuple-element.188, f32[128,1024]{1,0:T(8,128)S(1)} %get-tuple-element.161, f32[128]{0:T(128)S(1)} %exponential_add_fusion.2, ...), kind=kOutput, calls=%fused_computation.7.clone.1 | convolution fusion | flops 17833984 | bytes 810496 | tf_op jit(solution)/shard_map/while/body/eval_jaxpr/dot_general | solution.py:23
  63.5 1.3 %fusion.73 = (f32[128]{0:T(128)S(1)}, f32[128,1024]{1,0:T(8,128)S(1)}) fusion(bf16[8,1024,64]{2,1,0:T(8,128)(2,1)} %get-tuple-element.186, s32[]{:T(128)} %get-tuple-element.173, bf16[8,128,64]{1,2,0:T(8,128)(2,1)S(1)} %get-tuple-element.185, s32[128]{0:T(128)S(1)} %get-tuple-element.189, s32[1024]{0:T(1024)S(1)} %get-tuple-element.190, ...), kind=kOutput, calls=%fused_computation.83.clone.1 | convolution fusion | flops 17694592 | bytes 809984 | tf_op jit(solution)/shard_map/while/body/eval_jaxpr/dot_general | solution.py:15
  65.4 0.6 broadcast_maximum_fusion.2
  66.5 0.7 exponential_add_fusion.2
  67.1 1.4 %fusion.75 = bf16[8,128,64]{1,2,0:T(8,128)(2,1)S(1)} fusion(bf16[8,128,64]{1,2,0:T(8,128)(2,1)S(1)} %get-tuple-element.174, s32[]{:T(128)} %get-tuple-element.173, bf16[8,1024,64]{2,1,0:T(8,128)(2,1)} %get-tuple-element.188, f32[128,1024]{1,0:T(8,128)S(1)} %get-tuple-element.161, f32[128]{0:T(128)S(1)} %exponential_add_fusion.2, ...), kind=kOutput, calls=%fused_computation.7.clone.1 | convolution fusion | flops 17833984 | bytes 810496 | tf_op jit(solution)/shard_map/while/body/eval_jaxpr/dot_general | solution.py:23
  68.6 1.3 %fusion.73 = (f32[128]{0:T(128)S(1)}, f32[128,1024]{1,0:T(8,128)S(1)}) fusion(bf16[8,1024,64]{2,1,0:T(8,128)(2,1)} %get-tuple-element.186, s32[]{:T(128)} %get-tuple-element.173, bf16[8,128,64]{1,2,0:T(8,128)(2,1)S(1)} %get-tuple-element.185, s32[128]{0:T(128)S(1)} %get-tuple-element.189, s32[1024]{0:T(1024)S(1)} %get-tuple-element.190, ...), kind=kOutput, calls=%fused_computation.83.clone.1 | convolution fusion | flops 17694592 | bytes 809984 | tf_op jit(solution)/shard_map/while/body/eval_jaxpr/dot_general | solution.py:15
  70.5 0.6 broadcast_maximum_fusion.2
  71.5 0.7 exponential_add_fusion.2
  72.2 1.4 %fusion.75 = bf16[8,128,64]{1,2,0:T(8,128)(2,1)S(1)} fusion(bf16[8,128,64]{1,2,0:T(8,128)(2,1)S(1)} %get-tuple-element.174, s32[]{:T(128)} %get-tuple-element.173, bf16[8,1024,64]{2,1,0:T(8,128)(2,1)} %get-tuple-element.188, f32[128,1024]{1,0:T(8,128)S(1)} %get-tuple-element.161, f32[128]{0:T(128)S(1)} %exponential_add_fusion.2, ...), kind=kOutput, calls=%fused_computation.7.clone.1 | convolution fusion | flops 17833984 | bytes 810496 | tf_op jit(solution)/shard_map/while/body/eval_jaxpr/dot_general | solution.py:23
  73.6 1.3 %fusion.73 = (f32[128]{0:T(128)S(1)}, f32[128,1024]{1,0:T(8,128)S(1)}) fusion(bf16[8,1024,64]{2,1,0:T(8,128)(2,1)} %get-tuple-element.186, s32[]{:T(128)} %get-tuple-element.173, bf16[8,128,64]{1,2,0:T(8,128)(2,1)S(1)} %get-tuple-element.185, s32[128]{0:T(128)S(1)} %get-tuple-element.189, s32[1024]{0:T(1024)S(1)} %get-tuple-element.190, ...), kind=kOutput, calls=%fused_computation.83.clone.1 | convolution fusion | flops 17694592 | bytes 809984 | tf_op jit(solution)/shard_map/while/body/eval_jaxpr/dot_general | solution.py:15
  75.6 0.6 broadcast_maximum_fusion.2
  76.6 0.7 exponential_add_fusion.2
  77.3 1.4 %fusion.75 = bf16[8,128,64]{1,2,0:T(8,128)(2,1)S(1)} fusion(bf16[8,128,64]{1,2,0:T(8,128)(2,1)S(1)} %get-tuple-element.174, s32[]{:T(128)} %get-tuple-element.173, bf16[8,1024,64]{2,1,0:T(8,128)(2,1)} %get-tuple-element.188, f32[128,1024]{1,0:T(8,128)S(1)} %get-tuple-element.161, f32[128]{0:T(128)S(1)} %exponential_add_fusion.2, ...), kind=kOutput, calls=%fused_computation.7.clone.1 | convolution fusion | flops 17833984 | bytes 810496 | tf_op jit(solution)/shard_map/while/body/eval_jaxpr/dot_general | solution.py:23
  78.7 1.3 %fusion.73 = (f32[128]{0:T(128)S(1)}, f32[128,1024]{1,0:T(8,128)S(1)}) fusion(bf16[8,1024,64]{2,1,0:T(8,128)(2,1)} %get-tuple-element.186, s32[]{:T(128)} %get-tuple-element.173, bf16[8,128,64]{1,2,0:T(8,128)(2,1)S(1)} %get-tuple-element.185, s32[128]{0:T(128)S(1)} %get-tuple-element.189, s32[1024]{0:T(1024)S(1)} %get-tuple-element.190, ...), kind=kOutput, calls=%fused_computation.83.clone.1 | convolution fusion | flops 17694592 | bytes 809984 | tf_op jit(solution)/shard_map/while/body/eval_jaxpr/dot_general | solution.py:15
  81.7 0.7 exponential_add_fusion.2
  82.3 1.4 %fusion.75 = bf16[8,128,64]{1,2,0:T(8,128)(2,1)S(1)} fusion(bf16[8,128,64]{1,2,0:T(8,128)(2,1)S(1)} %get-tuple-element.174, s32[]{:T(128)} %get-tuple-element.173, bf16[8,1024,64]{2,1,0:T(8,128)(2,1)} %get-tuple-element.188, f32[128,1024]{1,0:T(8,128)S(1)} %get-tuple-element.161, f32[128]{0:T(128)S(1)} %exponential_add_fusion.2, ...), kind=kOutput, calls=%fused_computation.7.clone.1 | convolution fusion | flops 17833984 | bytes 810496 | tf_op jit(solution)/shard_map/while/body/eval_jaxpr/dot_general | solution.py:23
  83.8 1.3 %fusion.73 = (f32[128]{0:T(128)S(1)}, f32[128,1024]{1,0:T(8,128)S(1)}) fusion(bf16[8,1024,64]{2,1,0:T(8,128)(2,1)} %get-tuple-element.186, s32[]{:T(128)} %get-tuple-element.173, bf16[8,128,64]{1,2,0:T(8,128)(2,1)S(1)} %get-tuple-element.185, s32[128]{0:T(128)S(1)} %get-tuple-element.189, s32[1024]{0:T(1024)S(1)} %get-tuple-element.190, ...), kind=kOutput, calls=%fused_computation.83.clone.1 | convolution fusion | flops 17694592 | bytes 809984 | tf_op jit(solution)/shard_map/while/body/eval_jaxpr/dot_general | solution.py:15
  86.8 0.7 exponential_add_fusion.2
  87.4 1.4 %fusion.75 = bf16[8,128,64]{1,2,0:T(8,128)(2,1)S(1)} fusion(bf16[8,128,64]{1,2,0:T(8,128)(2,1)S(1)} %get-tuple-element.174, s32[]{:T(128)} %get-tuple-element.173, bf16[8,1024,64]{2,1,0:T(8,128)(2,1)} %get-tuple-element.188, f32[128,1024]{1,0:T(8,128)S(1)} %get-tuple-element.161, f32[128]{0:T(128)S(1)} %exponential_add_fusion.2, ...), kind=kOutput, calls=%fused_computation.7.clone.1 | convolution fusion | flops 17833984 | bytes 810496 | tf_op jit(solution)/shard_map/while/body/eval_jaxpr/dot_general | solution.py:23
  88.9 1.3 %fusion.73 = (f32[128]{0:T(128)S(1)}, f32[128,1024]{1,0:T(8,128)S(1)}) fusion(bf16[8,1024,64]{2,1,0:T(8,128)(2,1)} %get-tuple-element.186, s32[]{:T(128)} %get-tuple-element.173, bf16[8,128,64]{1,2,0:T(8,128)(2,1)S(1)} %get-tuple-element.185, s32[128]{0:T(128)S(1)} %get-tuple-element.189, s32[1024]{0:T(1024)S(1)} %get-tuple-element.190, ...), kind=kOutput, calls=%fused_computation.83.clone.1 | convolution fusion | flops 17694592 | bytes 809984 | tf_op jit(solution)/shard_map/while/body/eval_jaxpr/dot_general | solution.py:15
  91.8 0.7 exponential_add_fusion.2
  92.5 1.4 %fusion.75 = bf16[8,128,64]{1,2,0:T(8,128)(2,1)S(1)} fusion(bf16[8,128,64]{1,2,0:T(8,128)(2,1)S(1)} %get-tuple-element.174, s32[]{:T(128)} %get-tuple-element.173, bf16[8,1024,64]{2,1,0:T(8,128)(2,1)} %get-tuple-element.188, f32[128,1024]{1,0:T(8,128)S(1)} %get-tuple-element.161, f32[128]{0:T(128)S(1)} %exponential_add_fusion.2, ...), kind=kOutput, calls=%fused_computation.7.clone.1 | convolution fusion | flops 17833984 | bytes 810496 | tf_op jit(solution)/shard_map/while/body/eval_jaxpr/dot_general | solution.py:23
  93.9 1.3 %fusion.73 = (f32[128]{0:T(128)S(1)}, f32[128,1024]{1,0:T(8,128)S(1)}) fusion(bf16[8,1024,64]{2,1,0:T(8,128)(2,1)} %get-tuple-element.186, s32[]{:T(128)} %get-tuple-element.173, bf16[8,128,64]{1,2,0:T(8,128)(2,1)S(1)} %get-tuple-element.185, s32[128]{0:T(128)S(1)} %get-tuple-element.189, s32[1024]{0:T(1024)S(1)} %get-tuple-element.190, ...), kind=kOutput, calls=%fused_computation.83.clone.1 | convolution fusion | flops 17694592 | bytes 809984 | tf_op jit(solution)/shard_map/while/body/eval_jaxpr/dot_general | solution.py:15
  96.9 0.7 exponential_add_fusion.2
  97.6 1.4 %fusion.75 = bf16[8,128,64]{1,2,0:T(8,128)(2,1)S(1)} fusion(bf16[8,128,64]{1,2,0:T(8,128)(2,1)S(1)} %get-tuple-element.174, s32[]{:T(128)} %get-tuple-element.173, bf16[8,1024,64]{2,1,0:T(8,128)(2,1)} %get-tuple-element.188, f32[128,1024]{1,0:T(8,128)S(1)} %get-tuple-element.161, f32[128]{0:T(128)S(1)} %exponential_add_fusion.2, ...), kind=kOutput, calls=%fused_computation.7.clone.1 | convolution fusion | flops 17833984 | bytes 810496 | tf_op jit(solution)/shard_map/while/body/eval_jaxpr/dot_general | solution.py:23
  100.0 1.4 %reduce.9 = bf16[128,512]{1,0:T(8,128)(2,1)S(1)} reduce(bf16[128,1,512]{2,1,0:T(2,128)(2,1)S(1)} %bitcast.108, bf16[]{:T(256)} %broadcast.123), dimensions={1}, to_apply=%bitcast.90.reduce_sub_computation | reduce | bytes 262146
  101.5 16.7 %all_to_all.36 = bf16[8,2,4096]{2,1,0:T(2,128)(2,1)S(1)} all-to-all(bf16[8,2,4096]{2,1,0:T(2,128)(2,1)S(1)} %reshape.157), channel_id=1, replica_groups=mesh['tile'=64,'lev'=8] {'lev'}, dimensions={0} | all-to-all | bytes 262144 | tf_op jit(solution)/shard_map/all_to_all | solution.py:122
  118.4 1.0 multiply_reduce_fusion
  120.8 11.5 %all_to_all.37 = bf16[8,16,512]{2,1,0:T(8,128)(2,1)S(1)} all-to-all(bf16[8,16,512]{2,1,0:T(8,128)(2,1)S(1)} %fusion.19), channel_id=1, replica_groups=mesh['tile'=64,'lev'=8] {'lev'}, dimensions={0} | all-to-all | bytes 262144 | tf_op jit(solution)/shard_map/all_to_all | solution.py:124
  132.2 0.7 copy.52
  (64 shorter events, 14.8 us)
Async XLA Ops:
  0.0 120.2 %copy-start = (bf16[1024,512]{1,0:T(8,128)(2,1)S(1)}, bf16[1024,512]{1,0:T(8,128)(2,1)}, u32[]{:S(2)}) copy-start(bf16[1024,512]{1,0:T(8,128)(2,1)} %param.27) | copy-start | bytes 3145732
  0.0 37.1 %copy-start.3 = (bf16[1,128,512]{2,1,0:T(8,128)(2,1)S(1)}, bf16[1,128,512]{2,1,0:T(8,128)(2,1)}, u32[]{:S(2)}) copy-start(bf16[1,128,512]{2,1,0:T(8,128)(2,1)} %param.15) | copy-start | bytes 393220
  0.0 37.1 %copy-start.2 = (bf16[512,512]{1,0:T(8,128)(2,1)S(1)}, bf16[512,512]{1,0:T(8,128)(2,1)}, u32[]{:S(2)}) copy-start(bf16[512,512]{1,0:T(8,128)(2,1)} %param.19) | copy-start | bytes 1572868
  0.0 53.8 %copy-start.4 = (bf16[256,512]{1,0:T(8,128)(2,1)S(1)}, bf16[256,512]{1,0:T(8,128)(2,1)}, u32[]{:S(2)}) copy-start(bf16[256,512]{1,0:T(8,128)(2,1)} %param.20) | copy-start | bytes 786436
  9.0 21.5 %all-to-all-start.1 = ((bf16[64,1,16]{2,1,0:T(2,128)(2,1)}), bf16[64,1,16]{2,1,0:T(2,128)(2,1)S(1)}, u32[]{:S(2)}, u32[]{:S(2)}) async-start(bf16[64,1,16]{2,1,0:T(2,128)(2,1)} %all_to_all.31), calls=%async_computation.1 | async-start | bytes 65536 | tf_op jit(solution)/shard_map/all_to_all | solution.py:91
  30.5 23.3 %all-to-all-start = ((bf16[64,16,256]{2,1,0:T(8,128)(2,1)}), bf16[64,16,256]{2,1,0:T(8,128)(2,1)S(1)}, u32[]{:S(2)}, u32[]{:S(2)}) async-start(bf16[64,16,256]{2,1,0:T(8,128)(2,1)} %bitcast.8), calls=%async_computation | async-start | bytes 1048576 | tf_op jit(solution)/shard_map/all_to_all | solution.py:84
  53.8 2.3 %copy-start.5 = (bf16[256,512]{1,0:T(8,128)(2,1)S(1)}, bf16[256,512]{1,0:T(8,128)(2,1)}, u32[]{:S(2)}) copy-start(bf16[256,512]{1,0:T(8,128)(2,1)} %param.21) | copy-start | bytes 786436
  56.1 2.3 %copy-start.9 = (f32[8]{0:T(128)S(1)}, f32[8]{0:T(128)}, u32[]{:S(2)}) copy-start(f32[8]{0:T(128)} %param.23) | copy-start | bytes 100
  58.4 40.6 %copy-start.1 = (bf16[512,512]{1,0:T(8,128)(2,1)S(1)}, bf16[512,512]{1,0:T(8,128)(2,1)}, u32[]{:S(2)}) copy-start(bf16[512,512]{1,0:T(8,128)(2,1)} %param.22) | copy-start | bytes 1572868
  99.0 20.6 %copy-start.7 = (f32[512]{0:T(512)S(1)}, f32[512]{0:T(512)}, u32[]{:S(2)}) copy-start(f32[512]{0:T(512)} %param.24) | copy-start | bytes 6148
  99.0 20.6 %copy-start.6 = (f32[8,8]{1,0:T(8,128)S(1)}, f32[8,8]{1,0:T(8,128)}, u32[]{:S(2)}) copy-start(f32[8,8]{1,0:T(8,128)} %param.25) | copy-start | bytes 772
  99.3 20.9 %copy-start.8 = (bf16[512,1024]{1,0:T(8,128)(2,1)S(1)}, bf16[512,1024]{1,0:T(8,128)(2,1)}, u32[]{:S(2)}) copy-start(bf16[512,1024]{1,0:T(8,128)(2,1)} %param.26) | copy-start | bytes 3145732
where the time goes:
time: 134 us; the launch traced here: 133 us
  blocking collectives  28.2 us (21%)
  matrix products  24.7 us (18%)
  starting transfers between devices  20.6 us (15%)
  other arithmetic  20.5 us (15%)
  waiting for transfers between devices  19.8 us (15%)
  local copies, waits for them, and re-layouts  18.5 us (14%)
    all_to_all x1, blocking collectives, body(): lax.all_to_all(updated, 'lev', split_axis=1, concat_axis=0, tiled=True)  16.7 us
    all_to_all x1, waiting for transfers between devices, body(): lax.all_to_all(token_bank.reshape(tile_count, capacity, observations.shap...  15.9 us
    all_to_all x1, starting transfers between devices, body(): lax.all_to_all(slot_codes, 'tile', split_axis=0, concat_axis=0, tiled=True)  14 us
    all_to_all x1, blocking collectives, body(): lax.all_to_all(encoded, 'lev', split_axis=0, concat_axis=1, tiled=True)  11.5 us
    dot_general x8, matrix products, per_head(): jnp.dot(probability, v_head, preferred_element_type=jnp.float32)  11.3 us
    dot_general x8, matrix products, per_head(): jnp.dot(q_head, k_head.T, preferred_element_type=jnp.float32)  10.8 us
    all_to_all x1, starting transfers between devices, body(): lax.all_to_all(token_bank.reshape(tile_count, capacity, observations.shap...  6.56 us
    add x8, other arithmetic, per_head(): jnp.exp(sink_head - peak) + jnp.sum(weights, axis=1, keepdims=True)  5.28 us
  transfers between devices with their start and end apart: 2, of which 2 were waited for; matrix products, arithmetic and copies ran while one was open for 3% of the time, Pallas kernels for 0%

commit v1 on v0

v1 whole, which is shorter than its diff:
```python
import functools

import jax
import jax.numpy as jnp
from jax import lax
from jax.experimental import pallas as pl
from jax.experimental.pallas import tpu as pltpu
from jax.sharding import PartitionSpec as P

SUBCELLS = 32
HEADS = 8
EMPTY = 64.0
EMPTY_FROM = 48.0
MIB = 1 << 20


def route_kernel(sub_here, target_ref, subtile_ref, tokens_ref, bank_ref, *, tile_count, capacity):
    rows = tokens_ref.shape[0]
    width = tokens_ref.shape[1]
    keep = jnp.abs(subtile_ref[...] - sub_here[0]) <= 1
    target = jnp.where(keep, target_ref[...], -1)
    tile_ids = lax.broadcasted_iota(jnp.int32, (tile_count, rows), 0)
    named = target == tile_ids
    onehot = jnp.where(named, 1.0, 0.0)
    before = lax.broadcasted_iota(jnp.int32, (rows, rows), 0) < lax.broadcasted_iota(
        jnp.int32, (rows, rows), 1
    )
    before = jnp.where(before, 1.0, 0.0).astype(jnp.bfloat16)
    rank = jnp.dot(onehot.astype(jnp.bfloat16), before, preferred_element_type=jnp.float32)
    rank = jnp.where(named, rank, -1.0)
    count = jnp.sum(onehot, axis=1, keepdims=True)
    tokens = tokens_ref[...]
    group = 8
    slot = lax.broadcasted_iota(jnp.int32, (group, capacity, rows), 1).astype(jnp.float32)
    slot_out = lax.broadcasted_iota(jnp.int32, (group, capacity, width), 1).astype(jnp.float32)
    for first in range(0, tile_count, group):
        pick = jnp.where(rank[first : first + group][:, None, :] == slot, 1.0, 0.0)
        pick = pick.reshape(group * capacity, rows).astype(jnp.bfloat16)
        taken = jnp.dot(pick, tokens, preferred_element_type=jnp.float32)
        filled = slot_out < count[first : first + group][:, None, :]
        taken = jnp.where(filled, taken.reshape(group, capacity, width), EMPTY)
        bank_ref[first * capacity : (first + group) * capacity, :] = taken.reshape(
            group * capacity, width
        ).astype(jnp.bfloat16)


def encode_kernel(
    tokens_ref,
    query_ref,
    grid_ref,
    key_weight_ref,
    value_weight_ref,
    out_weight_ref,
    gain_ref,
    up_ref,
    down_ref,
    sink_ref,
    mixing_ref,
    encoded_ref,
    *,
    levels,
):
    rows, width = query_ref.shape
    head_width = width // HEADS
    pair = 2 * head_width
    tokens = tokens_ref[...]
    over_tokens = (((1,), (1,)), ((), ()))
    lane = lax.broadcasted_iota(jnp.int32, (16, tokens.shape[1]), 1)
    first_feature = jnp.where(lane == 0, 1.0, 0.0).astype(jnp.bfloat16)
    marks = lax.dot_general(
        first_feature, tokens, over_tokens, preferred_element_type=jnp.float32
    )[0:1]
    bias = jnp.where(marks > EMPTY_FROM, -1e30, 0.0)
    keys = lax.dot_general(
        key_weight_ref[...], tokens, over_tokens, preferred_element_type=jnp.float32
    ).astype(jnp.bfloat16)
    values = jnp.dot(tokens, value_weight_ref[...], preferred_element_type=jnp.float32).astype(
        jnp.bfloat16
    )
    left = lax.broadcasted_iota(jnp.int32, (rows, pair), 1) < head_width
    attended = []
    for p in range(HEADS // 2):
        lanes = slice(p * pair, (p + 1) * pair)
        query = query_ref[:, lanes].astype(jnp.float32) * head_width**-0.5
        both = jnp.concatenate(
            [jnp.where(left, query, 0.0), jnp.where(left, 0.0, query)], axis=0
        ).astype(jnp.bfloat16)
        scores = jnp.dot(both, keys[lanes], preferred_element_type=jnp.float32) + bias
        row_head = lax.broadcasted_iota(jnp.int32, (2 * rows, 1), 0) < rows
        sink = jnp.where(row_head, sink_ref[2 * p], sink_ref[2 * p + 1])
        peak = jnp.maximum(jnp.max(scores, axis=1, keepdims=True), sink)
        weights = jnp.exp(scores - peak)
        total = jnp.exp(sink - peak) + jnp.sum(weights, axis=1, keepdims=True)
        mixed = jnp.dot(
            weights.astype(jnp.bfloat16), values[:, lanes], preferred_element_type=jnp.float32
        )
        mixed = mixed / total
        attended.append(jnp.where(left, mixed[:rows], mixed[rows:]).astype(jnp.bfloat16))
    attended = jnp.concatenate(attended, axis=1)
    updated = (
        grid_ref[...].astype(jnp.float32)
        + jnp.dot(attended, out_weight_ref[...], preferred_element_type=jnp.float32)
    ).astype(jnp.bfloat16)
    wide = updated.astype(jnp.float32)
    inverse = lax.rsqrt(jnp.mean(wide * wide, axis=1, keepdims=True) + 1e-05)
    normed = wide * inverse * gain_ref[...]
    cells = rows // levels
    parts = [normed[m * cells : (m + 1) * cells] for m in range(levels)]
    blended = []
    for l in range(levels):
        total = mixing_ref[l, 0] * parts[0]
        for m in range(1, levels):
            total = total + mixing_ref[l, m] * parts[m]
        blended.append(total)
    blended = jnp.concatenate(blended, axis=0).astype(jnp.bfloat16)
    hidden = jax.nn.gelu(
        jnp.dot(blended, up_ref[...], preferred_element_type=jnp.float32)
    ).astype(jnp.bfloat16)
    encoded_ref[...] = (
        wide + jnp.dot(hidden, down_ref[...], preferred_element_type=jnp.float32)
    ).astype(jnp.bfloat16)


def body(
    grid_state,
    observations,
    destination,
    subtile,
    query_weight,
    key_weight,
    value_weight,
    out_weight,
    sink_logit,
    norm_gain,
    mixing,
    up_weight,
    down_weight,
):
    tile_count = lax.axis_size("tile")
    levels = lax.axis_size("lev")
    token_rows, token_width = observations.shape
    capacity = 2 * token_rows // tile_count
    cells, width = grid_state.shape[1:]
    cells_here = cells // levels
    rows = levels * cells_here
    sub_here = (lax.axis_index("lev") * cells_here // SUBCELLS).reshape(1)
    smem = pl.BlockSpec(memory_space=pltpu.SMEM)
    vmem = pl.BlockSpec(memory_space=pltpu.VMEM)

    columns = lax.all_to_all(
        grid_state.reshape(levels, cells_here, width), "lev", split_axis=0, concat_axis=0, tiled=True
    ).reshape(rows, width)
    bank = pl.pallas_call(
        functools.partial(route_kernel, tile_count=tile_count, capacity=capacity),
        out_shape=jax.ShapeDtypeStruct((tile_count * capacity, token_width), observations.dtype),
        in_specs=[smem, vmem, vmem, vmem],
        out_specs=vmem,
        compiler_params=pltpu.CompilerParams(vmem_limit_bytes=16 * MIB),
        cost_estimate=pl.CostEstimate(flops=300_000_000, bytes_accessed=MIB, transcendentals=0),
        name="route",
    )(
        sub_here,
        destination.reshape(1, token_rows),
        subtile.reshape(1, token_rows),
        observations,
    )
    received = lax.all_to_all(
        bank.reshape(tile_count, capacity, token_width),
        "tile",
        split_axis=0,
        concat_axis=0,
        tiled=True,
    ).reshape(tile_count * capacity, token_width)
    queries = jnp.dot(columns, query_weight, preferred_element_type=jnp.float32).astype(
        jnp.bfloat16
    )
    encoded = pl.pallas_call(
        functools.partial(encode_kernel, levels=levels),
        out_shape=jax.ShapeDtypeStruct((rows, width), jnp.bfloat16),
        in_specs=[vmem] * 9 + [smem, smem],
        out_specs=vmem,
        compiler_params=pltpu.CompilerParams(vmem_limit_bytes=32 * MIB),
        cost_estimate=pl.CostEstimate(
            flops=1_500_000_000, bytes_accessed=5 * MIB, transcendentals=1_200_000
        ),
        name="encode",
    )(
        received,
        queries,
        columns,
        key_weight.T,
        value_weight,
        out_weight,
        norm_gain.reshape(1, width),
        up_weight,
        down_weight,
        sink_logit,
        mixing,
    )
    return lax.all_to_all(
        encoded.reshape(levels, cells_here, width), "lev", split_axis=0, concat_axis=1, tiled=True
    )


def solution(mesh):
    placed = (
        P("lev", "tile", None),
        P("tile", None),
        P("tile", None),
        P("tile"),
        P(),
        P(),
        P(),
        P(),
        P(),
        P(),
        P(),
        P(),
        P(),
    )
    return jax.shard_map(
        body, mesh=mesh, in_specs=placed, out_specs=P("lev", "tile", None), check_vma=False
    )
```

time: 134 us -> 67.1 us (0.50)
  the two profiles are of different devices: /device:TPU:6 before, /device:TPU:7 now
where the time goes in v1:
time: 67.1 us; the launch traced here: 66.7 us
  starting transfers between devices  23 us (34%)
  waiting for transfers between devices  22.4 us (33%)
  blocking collectives  12 us (18%)
  Pallas kernels  5.67 us (8%)
  local copies, waits for them, and re-layouts  3.35 us (5%)
    all_to_all x1, waiting for transfers between devices, body(): lax.all_to_all(bank.reshape(tile_count, capacity, token_width), 'tile', s...  16.7 us
    all_to_all x1, starting transfers between devices, body(): lax.all_to_all(bank.reshape(tile_count, capacity, token_width), 'tile', s...  16.1 us
    all_to_all x1, blocking collectives, body(): lax.all_to_all(encoded.reshape(levels, cells_here, width), 'lev', split_a...  12 us
    all_to_all x1, starting transfers between devices, body(): lax.all_to_all(grid_state.reshape(levels, cells_here, width), 'lev', spli...  6.95 us
    all_to_all x1, waiting for transfers between devices, body(): lax.all_to_all(grid_state.reshape(levels, cells_here, width), 'lev', spli...  5.64 us
    pallas_call x1, Pallas kernels, body(): pl.pallas_call(functools.partial(encode_kernel, levels=levels), out_shape...  4.25 us
    unnamed x26, local copies, waits for them, and re-layouts  3.35 us
    pallas_call x1, Pallas kernels, body(): pl.pallas_call(functools.partial(route_kernel, tile_count=tile_count, cap...  1.43 us
  transfers between devices with their start and end apart: 2, of which 2 were waited for; matrix products, arithmetic and copies ran while one was open for 1% of the time, Pallas kernels for 2%

profile of v1, /device:TPU:7, one launch (start us, length us, event | category | flops | bytes accessed | tf_op | source)
XLA Modules:
  0.0 66.7 jit_solution(6698493537756804505)
XLA Ops:
  0.0 0.0 copy-start
  0.0 0.0 copy-start.4
  0.0 7.0 %all-to-all-start.1 = ((bf16[8,16,512]{2,1,0:T(8,128)(2,1)}), bf16[8,16,512]{2,1,0:T(8,128)(2,1)S(1)}, u32[]{:S(2)}, u32[]{:S(2)}) async-start(bf16[8,16,512]{2,1,0:T(8,128)(2,1)} %bitcast.22), calls=%async_computation.1 | async-start | bytes 262144 | tf_op jit(solution)/shard_map/all_to_all | solution.py:150
  7.0 0.0 copy-start.8
  7.0 0.0 copy-start.7
  7.0 0.0 copy-done.4
  7.0 0.7 copy-done.8
  7.6 0.0 copy-done.7
  7.7 0.0 copy-start.11
  7.7 1.4 %route.1 = bf16[1024,256]{1,0:T(8,128)(2,1)} custom-call(s32[1]{0:T(128)} %bitcast.sub_here, s32[1,512]{1,0:T(1,128)S(1)} %bitcast.18, s32[1,512]{1,0:T(1,128)S(1)} %bitcast.19, bf16[512,256]{1,0:T(8,128)(2,1)S(1)} %copy-done.4), custom_call_target="tpu_custom_call" | custom-call | flops 300000000 | bytes 1048576 | tf_op jit(solution)/shard_map/route/pallas_call | solution.py:153
  9.1 5.6 %all-to-all-done.1 = bf16[8,16,512]{2,1,0:T(8,128)(2,1)S(1)} async-done(((bf16[8,16,512]{2,1,0:T(8,128)(2,1)}), bf16[8,16,512]{2,1,0:T(8,128)(2,1)S(1)}, u32[]{:S(2)}, u32[]{:S(2)}) %all-to-all-start.1) | async-done | bytes 131104 | tf_op jit(solution)/shard_map/all_to_all | solution.py:150
  14.7 0.0 copy-start.1
  14.7 16.1 %all-to-all-start = ((bf16[64,16,256]{2,1,0:T(8,128)(2,1)}), bf16[64,16,256]{2,1,0:T(8,128)(2,1)S(1)}, u32[]{:S(2)}, u32[]{:S(2)}) async-start(bf16[64,16,256]{2,1,0:T(8,128)(2,1)} %bitcast.3), calls=%async_computation | async-start | bytes 1048576 | tf_op jit(solution)/shard_map/all_to_all | solution.py:167
  30.8 0.0 copy-done.11
  30.8 0.1 copy.14
  31.0 0.0 copy-start.3
  31.0 0.0 copy-done
  31.0 0.0 copy-start.5
  31.0 0.0 copy-start.9
  31.0 0.2 convolution_convert_fusion.query_ref
  31.2 0.0 copy-start.6
  31.3 16.7 %all-to-all-done = bf16[64,16,256]{2,1,0:T(8,128)(2,1)S(1)} async-done(((bf16[64,16,256]{2,1,0:T(8,128)(2,1)}), bf16[64,16,256]{2,1,0:T(8,128)(2,1)S(1)}, u32[]{:S(2)}, u32[]{:S(2)}) %all-to-all-start) | async-done | bytes 524320 | tf_op jit(solution)/shard_map/all_to_all | solution.py:167
  48.0 0.0 copy-start.10
  48.0 0.0 copy-done.1
  48.0 0.0 copy-done.3
  48.0 0.0 copy-done.5
  48.0 0.0 copy-done.9
  48.0 0.0 copy-done.6
  48.0 0.6 copy-done.10
  48.6 0.0 copy-start.2
  48.6 1.2 %copy-done.2 = bf16[1024,512]{1,0:T(8,128)(2,1)S(1)} copy-done((bf16[1024,512]{1,0:T(8,128)(2,1)S(1)}, bf16[1024,512]{1,0:T(8,128)(2,1)}, u32[]{:S(2)}) %copy-start.2) | copy-done | bytes 1048600
  49.9 4.2 %encode.1 = bf16[128,512]{1,0:T(8,128)(2,1)S(1)} custom-call(bf16[1024,256]{1,0:T(8,128)(2,1)S(1)} %bitcast.13, bf16[128,512]{1,0:T(8,128)(2,1)S(1)} %convolution_convert_fusion.query_ref, bf16[128,512]{1,0:T(8,128)(2,1)S(1)} %bitcast.15, bf16[512,256]{1,0:T(8,128)(2,1)S(1)} %bitcast.16, bf16[256,512]{1,0:T(8,128)(2,1)S(1)} %copy-done.5, ...), custom_call_target="tpu_custom_call" | custom-call | flops 1500000000 | bytes 5242880 | tf_op jit(solution)/shard_map/encode/pallas_call | solution.py:177
  54.1 12.0 %all_to_all.22 = bf16[8,16,512]{2,1,0:T(8,128)(2,1)S(1)} all-to-all(bf16[8,16,512]{2,1,0:T(8,128)(2,1)S(1)} %bitcast.17), channel_id=1, replica_groups=mesh['tile'=64,'lev'=8] {'lev'}, dimensions={0} | all-to-all | bytes 262144 | tf_op jit(solution)/shard_map/all_to_all | solution.py:200
  66.1 0.7 copy.16
Async XLA Ops:
  0.0 31.0 %copy-start = (bf16[512,512]{1,0:T(8,128)(2,1)S(1)}, bf16[512,512]{1,0:T(8,128)(2,1)}, u32[]{:S(2)}) copy-start(bf16[512,512]{1,0:T(8,128)(2,1)} %param.17) | copy-start | bytes 1572868
  0.0 7.0 %copy-start.4 = (bf16[512,256]{1,0:T(8,128)(2,1)S(1)}, bf16[512,256]{1,0:T(8,128)(2,1)}, u32[]{:S(2)}) copy-start(bf16[512,256]{1,0:T(8,128)(2,1)} %tokens_ref.1) | copy-start | bytes 786436
  0.0 14.7 %all-to-all-start.1 = ((bf16[8,16,512]{2,1,0:T(8,128)(2,1)}), bf16[8,16,512]{2,1,0:T(8,128)(2,1)S(1)}, u32[]{:S(2)}, u32[]{:S(2)}) async-start(bf16[8,16,512]{2,1,0:T(8,128)(2,1)} %bitcast.22), calls=%async_computation.1 | async-start | bytes 262144 | tf_op jit(solution)/shard_map/all_to_all | solution.py:150
  7.0 0.7 %copy-start.8 = (s32[512]{0:T(512)S(1)}, s32[512]{0:T(512)}, u32[]{:S(2)}) copy-start(s32[512]{0:T(512)} %param.16) | copy-start | bytes 6148
  7.0 0.7 %copy-start.7 = (s32[512,1]{0,1:T(1,128)S(1)}, s32[512,1]{0,1:T(1,128)}, u32[]{:S(2)}) copy-start(s32[512,1]{0,1:T(1,128)} %param.15) | copy-start | bytes 6148
  7.7 23.2 %copy-start.11 = (bf16[256,512]{1,0:T(8,128)(2,1)S(1)}, bf16[256,512]{1,0:T(8,128)(2,1)}, u32[]{:S(2)}) copy-start(bf16[256,512]{1,0:T(8,128)(2,1)} %param.18) | copy-start | bytes 786436
  14.7 33.3 %copy-start.1 = (bf16[512,1024]{1,0:T(8,128)(2,1)S(1)}, bf16[512,1024]{1,0:T(8,128)(2,1)}, u32[]{:S(2)}) copy-start(bf16[512,1024]{1,0:T(8,128)(2,1)} %up_ref.1) | copy-start | bytes 3145732
  14.7 33.2 %all-to-all-start = ((bf16[64,16,256]{2,1,0:T(8,128)(2,1)}), bf16[64,16,256]{2,1,0:T(8,128)(2,1)S(1)}, u32[]{:S(2)}, u32[]{:S(2)}) async-start(bf16[64,16,256]{2,1,0:T(8,128)(2,1)} %bitcast.3), calls=%async_computation | async-start | bytes 1048576 | tf_op jit(solution)/shard_map/all_to_all | solution.py:167
  31.0 17.0 %copy-start.3 = (bf16[512,512]{1,0:T(8,128)(2,1)S(1)}, bf16[512,512]{1,0:T(8,128)(2,1)}, u32[]{:S(2)}) copy-start(bf16[512,512]{1,0:T(8,128)(2,1)} %out_weight_ref.1) | copy-start | bytes 1572868
  31.0 17.0 %copy-start.5 = (bf16[256,512]{1,0:T(8,128)(2,1)S(1)}, bf16[256,512]{1,0:T(8,128)(2,1)}, u32[]{:S(2)}) copy-start(bf16[256,512]{1,0:T(8,128)(2,1)} %value_weight_ref.1) | copy-start | bytes 786436
  31.0 17.0 %copy-start.9 = (f32[512]{0:T(512)S(1)}, f32[512]{0:T(512)}, u32[]{:S(2)}) copy-start(f32[512]{0:T(512)} %param.22) | copy-start | bytes 6148
  31.2 16.8 %copy-start.6 = (f32[8,8]{1,0:T(8,128)S(1)}, f32[8,8]{1,0:T(8,128)}, u32[]{:S(2)}) copy-start(f32[8,8]{1,0:T(8,128)} %mixing_ref.1) | copy-start | bytes 772
  48.0 0.7 copy-start.10
  48.6 1.2 %copy-start.2 = (bf16[1024,512]{1,0:T(8,128)(2,1)S(1)}, bf16[1024,512]{1,0:T(8,128)(2,1)}, u32[]{:S(2)}) copy-start(bf16[1024,512]{1,0:T(8,128)(2,1)} %down_ref.1) | copy-start | bytes 3145732

commit v2 on v1

--- a/solution.py
+++ b/solution.py
@@ -14,21 +14,55 @@
 MIB = 1 << 20
 
 
-def route_kernel(sub_here, target_ref, subtile_ref, tokens_ref, bank_ref, *, tile_count, capacity):
+FIRST = 1
+LATER = (0, 5, 6, 2)
+
+
+def pick(pieces, levels):
+    return jnp.stack([lax.dynamic_index_in_dim(pieces, l, 0, keepdims=False) for l in levels])
+
+
+def start_loads(far, near, loaded):
+    loads = [pltpu.make_async_copy(f, n, loaded.at[i]) for i, (f, n) in enumerate(zip(far, near))]
+    for load in loads:
+        load.start()
+    return loads
+
+
+def route_kernel(
+    sub_here,
+    target_hbm,
+    subtile_hbm,
+    tokens_hbm,
+    bank_ref,
+    target_ref,
+    subtile_ref,
+    tokens_ref,
+    loaded,
+    *,
+    tile_count,
+    capacity,
+):
+    loads = start_loads(
+        (target_hbm, subtile_hbm, tokens_hbm), (target_ref, subtile_ref, tokens_ref), loaded
+    )
     rows = tokens_ref.shape[0]
     width = tokens_ref.shape[1]
+    before = lax.broadcasted_iota(jnp.int32, (rows, rows), 0) < lax.broadcasted_iota(
+        jnp.int32, (rows, rows), 1
+    )
+    before = jnp.where(before, 1.0, 0.0).astype(jnp.bfloat16)
+    loads[0].wait()
+    loads[1].wait()
     keep = jnp.abs(subtile_ref[...] - sub_here[0]) <= 1
     target = jnp.where(keep, target_ref[...], -1)
     tile_ids = lax.broadcasted_iota(jnp.int32, (tile_count, rows), 0)
     named = target == tile_ids
     onehot = jnp.where(named, 1.0, 0.0)
-    before = lax.broadcasted_iota(jnp.int32, (rows, rows), 0) < lax.broadcasted_iota(
-        jnp.int32, (rows, rows), 1
-    )
-    before = jnp.where(before, 1.0, 0.0).astype(jnp.bfloat16)
     rank = jnp.dot(onehot.astype(jnp.bfloat16), before, preferred_element_type=jnp.float32)
     rank = jnp.where(named, rank, -1.0)
     count = jnp.sum(onehot, axis=1, keepdims=True)
+    loads[2].wait()
     tokens = tokens_ref[...]
     group = 8
     slot = lax.broadcasted_iota(jnp.int32, (group, capacity, rows), 1).astype(jnp.float32)
@@ -44,22 +78,32 @@
         ).astype(jnp.bfloat16)
 
 
-def encode_kernel(
-    tokens_ref,
-    query_ref,
-    grid_ref,
-    key_weight_ref,
-    value_weight_ref,
-    out_weight_ref,
-    gain_ref,
-    up_ref,
-    down_ref,
-    sink_ref,
-    mixing_ref,
-    encoded_ref,
-    *,
-    levels,
-):
+def stage_kernel(key_ref, key_columns_ref):
+    key_columns_ref[...] = key_ref[...].astype(jnp.float32).T.astype(jnp.bfloat16)
+
+
+def query_kernel(*refs):
+    *piece_refs, weight_ref, columns_ref, query_ref = refs
+    columns = jnp.concatenate([ref[...] for ref in piece_refs], axis=0)
+    columns_ref[...] = columns
+    query = jnp.dot(columns, weight_ref[...], preferred_element_type=jnp.float32)
+    query_ref[...] = query.astype(jnp.bfloat16)
+
+
+def encode_kernel(*refs, block_order):
+    level_here, tokens_ref, key_weight_ref, query_ref, grid_ref = refs[:5]
+    far, encoded_ref, near, loaded = refs[5:12], refs[12], refs[13:20], refs[20]
+    (
+        value_weight_ref,
+        sink_ref,
+        out_weight_ref,
+        gain_ref,
+        mixing_ref,
+        up_ref,
+        down_ref,
+    ) = near
+    loads = start_loads(far, near, loaded)
+    levels = len(block_order)
     rows, width = query_ref.shape
     head_width = width // HEADS
     pair = 2 * head_width
@@ -74,6 +118,8 @@
     keys = lax.dot_general(
         key_weight_ref[...], tokens, over_tokens, preferred_element_type=jnp.float32
     ).astype(jnp.bfloat16)
+    loads[0].wait()
+    loads[1].wait()
     values = jnp.dot(tokens, value_weight_ref[...], preferred_element_type=jnp.float32).astype(
         jnp.bfloat16
     )
@@ -97,6 +143,8 @@
         mixed = mixed / total
         attended.append(jnp.where(left, mixed[:rows], mixed[rows:]).astype(jnp.bfloat16))
     attended = jnp.concatenate(attended, axis=1)
+    for load in loads[2:5]:
+        load.wait()
     updated = (
         grid_ref[...].astype(jnp.float32)
         + jnp.dot(attended, out_weight_ref[...], preferred_element_type=jnp.float32)
@@ -106,19 +154,29 @@
     normed = wide * inverse * gain_ref[...]
     cells = rows // levels
     parts = [normed[m * cells : (m + 1) * cells] for m in range(levels)]
+    held = [level_here[0] ^ offset for offset in block_order]
     blended = []
-    for l in range(levels):
-        total = mixing_ref[l, 0] * parts[0]
+    for l in held:
+        total = mixing_ref[l, held[0]] * parts[0]
         for m in range(1, levels):
-            total = total + mixing_ref[l, m] * parts[m]
+            total = total + mixing_ref[l, held[m]] * parts[m]
         blended.append(total)
     blended = jnp.concatenate(blended, axis=0).astype(jnp.bfloat16)
+    loads[5].wait()
     hidden = jax.nn.gelu(
         jnp.dot(blended, up_ref[...], preferred_element_type=jnp.float32)
     ).astype(jnp.bfloat16)
-    encoded_ref[...] = (
+    loads[6].wait()
+    encoded = (
         wide + jnp.dot(hidden, down_ref[...], preferred_element_type=jnp.float32)
     ).astype(jnp.bfloat16)
+    for e, l in enumerate(held):
+        start = pl.multiple_of(l * cells, cells)
+        encoded_ref[pl.ds(start, cells), :] = encoded[e * cells : (e + 1) * cells]
+
+
+def exchange_permute(array, offset, count):
+    return lax.ppermute(array, "lev", [(i, i ^ offset) for i in range(count)])
 
 
 def body(
@@ -146,24 +204,37 @@
     sub_here = (lax.axis_index("lev") * cells_here // SUBCELLS).reshape(1)
     smem = pl.BlockSpec(memory_space=pltpu.SMEM)
     vmem = pl.BlockSpec(memory_space=pltpu.VMEM)
-
-    columns = lax.all_to_all(
-        grid_state.reshape(levels, cells_here, width), "lev", split_axis=0, concat_axis=0, tiled=True
-    ).reshape(rows, width)
+    far = pl.BlockSpec(memory_space=pl.ANY)
+
+    here = lax.axis_index("lev")
+    pieces = grid_state.reshape(levels, cells_here, width)
+    came = exchange_permute(pick(pieces, [here ^ FIRST ^ o for o in LATER]), FIRST, levels)
     bank = pl.pallas_call(
         functools.partial(route_kernel, tile_count=tile_count, capacity=capacity),
         out_shape=jax.ShapeDtypeStruct((tile_count * capacity, token_width), observations.dtype),
-        in_specs=[smem, vmem, vmem, vmem],
+        in_specs=[smem, far, far, far],
         out_specs=vmem,
-        compiler_params=pltpu.CompilerParams(vmem_limit_bytes=16 * MIB),
+        scratch_shapes=[
+            pltpu.VMEM((1, token_rows), jnp.int32),
+            pltpu.VMEM((1, token_rows), jnp.int32),
+            pltpu.VMEM(observations.shape, observations.dtype),
+            pltpu.SemaphoreType.DMA((3,)),
+        ],
+        compiler_params=pltpu.CompilerParams(vmem_limit_bytes=32 * MIB),
         cost_estimate=pl.CostEstimate(flops=300_000_000, bytes_accessed=MIB, transcendentals=0),
         name="route",
     )(
         sub_here,
-        destination.reshape(1, token_rows),
-        subtile.reshape(1, token_rows),
-        observations,
-    )
+        *(
+            pltpu.with_memory_space_constraint(o, pltpu.HBM)
+            for o in (
+                destination.reshape(1, token_rows),
+                subtile.reshape(1, token_rows),
+                observations,
+            )
+        ),
+    )
+    bank, came = lax.optimization_barrier((bank, came))
     received = lax.all_to_all(
         bank.reshape(tile_count, capacity, token_width),
         "tile",
@@ -171,32 +242,57 @@
         concat_axis=0,
         tiled=True,
     ).reshape(tile_count * capacity, token_width)
-    queries = jnp.dot(columns, query_weight, preferred_element_type=jnp.float32).astype(
-        jnp.bfloat16
-    )
+    key_columns = pl.pallas_call(
+        stage_kernel,
+        out_shape=jax.ShapeDtypeStruct(key_weight.shape[::-1], key_weight.dtype),
+        in_specs=[vmem],
+        out_specs=vmem,
+        compiler_params=pltpu.CompilerParams(vmem_limit_bytes=8 * MIB),
+        cost_estimate=pl.CostEstimate(flops=1000, bytes_accessed=MIB, transcendentals=0),
+        name="stage",
+    )(key_weight)
+    parts = []
+    for came_block, offset in zip(came, LATER):
+        both = jnp.stack([pick(pieces, [here ^ offset])[0], came_block])
+        both = both.reshape(2 * cells_here, width)
+        parts.append(both if offset == 0 else exchange_permute(both, offset, levels))
+    columns, queries = pl.pallas_call(
+        query_kernel,
+        out_shape=[jax.ShapeDtypeStruct((rows, width), jnp.bfloat16)] * 2,
+        in_specs=[vmem] * (len(parts) + 1),
+        out_specs=[vmem] * 2,
+        compiler_params=pltpu.CompilerParams(vmem_limit_bytes=8 * MIB),
+        cost_estimate=pl.CostEstimate(flops=67_000_000, bytes_accessed=MIB, transcendentals=0),
+        name="query",
+    )(*parts, query_weight)
+    operands = [
+        value_weight,
+        sink_logit,
+        out_weight,
+        norm_gain.reshape(1, width),
+        mixing,
+        up_weight,
+        down_weight,
+    ]
+    operands = [pltpu.with_memory_space_constraint(o, pltpu.HBM) for o in operands]
     encoded = pl.pallas_call(
-        functools.partial(encode_kernel, levels=levels),
+        functools.partial(
+            encode_kernel, block_order=[o ^ first for o in LATER for first in (0, FIRST)]
+        ),
         out_shape=jax.ShapeDtypeStruct((rows, width), jnp.bfloat16),
-        in_specs=[vmem] * 9 + [smem, smem],
+        in_specs=[smem] + [vmem] * 4 + [far] * len(operands),
         out_specs=vmem,
+        scratch_shapes=[
+            (pltpu.SMEM if operand.shape[-1] == HEADS else pltpu.VMEM)(operand.shape, operand.dtype)
+            for operand in operands
+        ]
+        + [pltpu.SemaphoreType.DMA((len(operands),))],
         compiler_params=pltpu.CompilerParams(vmem_limit_bytes=32 * MIB),
         cost_estimate=pl.CostEstimate(
             flops=1_500_000_000, bytes_accessed=5 * MIB, transcendentals=1_200_000
         ),
         name="encode",
-    )(
-        received,
-        queries,
-        columns,
-        key_weight.T,
-        value_weight,
-        out_weight,
-        norm_gain.reshape(1, width),
-        up_weight,
-        down_weight,
-        sink_logit,
-        mixing,
-    )
+    )(here.reshape(1), received, key_columns, queries, columns, *operands)
     return lax.all_to_all(
         encoded.reshape(levels, cells_here, width), "lev", split_axis=0, concat_axis=1, tiled=True
     )

time: 67.1 us -> 60.9 us (0.908)
  the two profiles are of different devices: /device:TPU:7 before, /device:TPU:6 now
where the time goes in v2:
time: 60.9 us; the launch traced here: 60.4 us
  starting transfers between devices  30 us (49%)
  blocking collectives  15.9 us (26%)
  Pallas kernels  7.72 us (13%)
  waiting for transfers between devices  5.05 us (8%)
  local copies, waits for them, and re-layouts  1.52 us (2%)
    all_to_all x1, blocking collectives, body(): lax.all_to_all(encoded.reshape(levels, cells_here, width), 'lev', split_a...  15.9 us
    ppermute x4, starting transfers between devices, exchange_permute(): return lax.ppermute(array, 'lev', [(i, i ^ offset) for i in range(count)])  15.8 us
    all_to_all x1, starting transfers between devices, body(): lax.all_to_all(bank.reshape(tile_count, capacity, token_width), 'tile', s...  14.1 us
    pallas_call x1, Pallas kernels, body(): pl.pallas_call(functools.partial(encode_kernel, block_order=[o ^ first fo...  5.08 us
    ppermute x4, waiting for transfers between devices, exchange_permute(): return lax.ppermute(array, 'lev', [(i, i ^ offset) for i in range(count)])  5.05 us
    pallas_call x1, Pallas kernels, body(): pl.pallas_call(functools.partial(route_kernel, tile_count=tile_count, cap...  2.27 us
  transfers between devices with their start and end apart: 5, of which 3 were waited for; matrix products, arithmetic and copies ran while one was open for 0% of the time, Pallas kernels for 4%

profile of v2, /device:TPU:6, one launch (start us, length us, event | category | flops | bytes accessed | tf_op | source)
XLA Modules:
  0.0 60.4 jit_solution(14159865957892878371)
XLA Ops:
  0.0 0.8 %constant_dynamic-slice_fusion = (bf16[1,16,512]{2,1,0:T(8,128)(2,1)S(1)}, bf16[1,16,512]{2,1,0:T(8,128)(2,1)S(1)}, bf16[1,16,512]{2,1,0:T(8,128)(2,1)S(1)}, bf1...) fusion(bf16[8,16,512]{2,1,0:T(8,128)(2,1)} %bitcast.18, ...), kind=kLoop, calls=%fused_computation.5 | loop fusion | bytes 262176 | tf_op jit(solution)/shard_map/jit(dynamic_index_in_dim)/dynamic_slice | solution.py:22
  0.9 3.5 %collective-permute-start = (bf16[4,16,512]{2,1,0:T(8,128)(2,1)S(1)}, bf16[4,16,512]{2,1,0:T(8,128)(2,1)S(1)}, u32[]{:S(2)}, u32[]{:S(2)}) collective-permute-start(bf16[4,16,512]{2,1,0:T(8,128)(2,1)S(1)} %pad_maximum_fusion), channel_id=1, source_target_pairs={{0,1},{1,0},{2,3},{3,2},{4,5},{5,4},{6,7},{7,6},{8,9},{9,8},{10,11... | collective-permute-start | bytes 196616 | tf_op jit(solution)/shard_map/ppermute | solution.py:179
  4.4 2.3 %route.1 = bf16[1024,256]{1,0:T(8,128)(2,1)} custom-call(s32[1]{0:T(128)} %bitcast.1.sub_here, s32[1,512]{1,0:T(1,128)} %bitcast.22, s32[1,512]{1,0:T(1,128)} %bitcast.23, bf16[512,256]{1,0:T(8,128)(2,1)} %tokens_hbm.1), custom_call_target="tpu_custom_call" | custom-call | flops 300000000 | bytes 1048576 | tf_op jit(solution)/shard_map/route/pallas_call | solution.py:212
  6.7 0.4 collective-permute-done
  7.0 0.0 copy-start.1
  7.0 14.1 %all-to-all-start = ((bf16[64,16,256]{2,1,0:T(8,128)(2,1)}), bf16[64,16,256]{2,1,0:T(8,128)(2,1)S(1)}, u32[]{:S(2)}, u32[]{:S(2)}) async-start(bf16[64,16,256]{2,1,0:T(8,128)(2,1)} %bitcast.5), calls=%async_computation | async-start | bytes 1048576 | tf_op jit(solution)/shard_map/all_to_all | solution.py:238
  21.2 0.0 copy-done.1
  21.2 0.0 copy-start
  21.2 0.1 stage.1.refs_2_
  21.4 6.9 %collective-permute-start.1 = (bf16[32,512]{1,0:T(8,128)(2,1)S(1)}, bf16[32,512]{1,0:T(8,128)(2,1)S(1)}, u32[]{:S(2)}, u32[]{:S(2)}) collective-permute-start(bf16[32,512]{1,0:T(8,128)(2,1)S(1)} %bitcast.19), channel_id=1, source_target_pairs={{0,5},{1,4},{2,7},{3,6},{4,1},{5,0},{6,3},{7,2},{8,13},{9,12},{10,... | collective-permute-start | bytes 98312 | tf_op jit(solution)/shard_map/ppermute | solution.py:179
  28.4 3.2 %collective-permute-start.2 = (bf16[32,512]{1,0:T(8,128)(2,1)S(1)}, bf16[32,512]{1,0:T(8,128)(2,1)S(1)}, u32[]{:S(2)}, u32[]{:S(2)}) collective-permute-start(bf16[32,512]{1,0:T(8,128)(2,1)S(1)} %bitcast.20), channel_id=1, source_target_pairs={{0,6},{1,7},{2,4},{3,5},{4,2},{5,3},{6,0},{7,1},{8,14},{9,15},{10,... | collective-permute-start | bytes 98312 | tf_op jit(solution)/shard_map/ppermute | solution.py:179
  31.5 2.2 %collective-permute-start.3 = (bf16[32,512]{1,0:T(8,128)(2,1)S(1)}, bf16[32,512]{1,0:T(8,128)(2,1)S(1)}, u32[]{:S(2)}, u32[]{:S(2)}) collective-permute-start(bf16[32,512]{1,0:T(8,128)(2,1)S(1)} %bitcast.21), channel_id=1, source_target_pairs={{0,2},{1,3},{2,0},{3,1},{4,6},{5,7},{6,4},{7,5},{8,10},{9,11},{10,... | collective-permute-start | bytes 98312 | tf_op jit(solution)/shard_map/ppermute | solution.py:179
  33.8 0.0 collective-permute-done.1.refs_1_
  33.8 2.5 %collective-permute-done.2.refs_2_ = bf16[32,512]{1,0:T(8,128)(2,1)S(1)} collective-permute-done((bf16[32,512]{1,0:T(8,128)(2,1)S(1)}, bf16[32,512]{1,0:T(8,128)(2,1)S(1)}, u32[]{:S(2)}, u32[]{:S(2)}) %collective-permute-start.2) | collective-permute-done | bytes 32800 | tf_op jit(solution)/shard_map/ppermute | solution.py:179
  36.3 2.2 %collective-permute-done.3.refs_3_ = bf16[32,512]{1,0:T(8,128)(2,1)S(1)} collective-permute-done((bf16[32,512]{1,0:T(8,128)(2,1)S(1)}, bf16[32,512]{1,0:T(8,128)(2,1)S(1)}, u32[]{:S(2)}, u32[]{:S(2)}) %collective-permute-start.3) | collective-permute-done | bytes 32800 | tf_op jit(solution)/shard_map/ppermute | solution.py:179
  38.5 0.0 copy-done
  38.5 0.2 query.1
  38.7 0.0 all-to-all-done
  38.7 5.1 %encode.1 = bf16[128,512]{1,0:T(8,128)(2,1)S(1)} custom-call(s32[1]{0:T(128)} %bitcast.refs_0_, bf16[1024,256]{1,0:T(8,128)(2,1)S(1)} %bitcast.14, bf16[512,256]{1,0:T(8,128)(2,1)S(1)} %stage.1.refs_2_, bf16[128,512]{1,0:T(8,128)(2,1)S(1)} %get-tuple-element.11.refs_3_, bf16[128,512]{1,0:T(8,128)(2,1)S(1)} %get-tuple-element.12.refs_4_, ...), custom_call_target="tpu_custom_call" | custom-call | flops 1500000000 | bytes 5242880 | tf_op jit(solution)/shard_map/encode/pallas_call | solution.py:278
  43.8 15.9 %all_to_all.17 = bf16[8,16,512]{2,1,0:T(8,128)(2,1)S(1)} all-to-all(bf16[8,16,512]{2,1,0:T(8,128)(2,1)S(1)} %bitcast.16), channel_id=1, replica_groups=mesh['tile'=64,'lev'=8] {'lev'}, dimensions={0} | all-to-all | bytes 262144 | tf_op jit(solution)/shard_map/all_to_all | solution.py:296
  59.7 0.7 %copy.15 = bf16[1,128,512]{2,1,0:T(8,128)(2,1)} copy(bf16[1,128,512]{2,1,0:T(8,128)(2,1)S(1)} %bitcast.17) | data formatting | bytes 262144
  (6 shorter events, 0.0 us)
Async XLA Ops:
  0.9 6.2 %collective-permute-start = (bf16[4,16,512]{2,1,0:T(8,128)(2,1)S(1)}, bf16[4,16,512]{2,1,0:T(8,128)(2,1)S(1)}, u32[]{:S(2)}, u32[]{:S(2)}) collective-permute-start(bf16[4,16,512]{2,1,0:T(8,128)(2,1)S(1)} %pad_maximum_fusion), channel_id=1, source_target_pairs={{0,1},{1,0},{2,3},{3,2},{4,5},{5,4},{6,7},{7,6},{8,9},{9,8},{10,11... | collective-permute-start | bytes 196616 | tf_op jit(solution)/shard_map/ppermute | solution.py:179
  7.0 14.2 %copy-start.1 = (bf16[256,512]{1,0:T(8,128)(2,1)S(1)}, bf16[256,512]{1,0:T(8,128)(2,1)}, u32[]{:S(2)}) copy-start(bf16[256,512]{1,0:T(8,128)(2,1)} %key_ref.1) | copy-start | bytes 786436
  7.0 31.7 %all-to-all-start = ((bf16[64,16,256]{2,1,0:T(8,128)(2,1)}), bf16[64,16,256]{2,1,0:T(8,128)(2,1)S(1)}, u32[]{:S(2)}, u32[]{:S(2)}) async-start(bf16[64,16,256]{2,1,0:T(8,128)(2,1)} %bitcast.5), calls=%async_computation | async-start | bytes 1048576 | tf_op jit(solution)/shard_map/all_to_all | solution.py:238
  21.2 17.3 %copy-start = (bf16[512,512]{1,0:T(8,128)(2,1)S(1)}, bf16[512,512]{1,0:T(8,128)(2,1)}, u32[]{:S(2)}) copy-start(bf16[512,512]{1,0:T(8,128)(2,1)} %refs_4_.1) | copy-start | bytes 1572868
  21.4 12.4 %collective-permute-start.1 = (bf16[32,512]{1,0:T(8,128)(2,1)S(1)}, bf16[32,512]{1,0:T(8,128)(2,1)S(1)}, u32[]{:S(2)}, u32[]{:S(2)}) collective-permute-start(bf16[32,512]{1,0:T(8,128)(2,1)S(1)} %bitcast.19), channel_id=1, source_target_pairs={{0,5},{1,4},{2,7},{3,6},{4,1},{5,0},{6,3},{7,2},{8,13},{9,12},{10,... | collective-permute-start | bytes 98312 | tf_op jit(solution)/shard_map/ppermute | solution.py:179
  28.4 7.9 %collective-permute-start.2 = (bf16[32,512]{1,0:T(8,128)(2,1)S(1)}, bf16[32,512]{1,0:T(8,128)(2,1)S(1)}, u32[]{:S(2)}, u32[]{:S(2)}) collective-permute-start(bf16[32,512]{1,0:T(8,128)(2,1)S(1)} %bitcast.20), channel_id=1, source_target_pairs={{0,6},{1,7},{2,4},{3,5},{4,2},{5,3},{6,0},{7,1},{8,14},{9,15},{10,... | collective-permute-start | bytes 98312 | tf_op jit(solution)/shard_map/ppermute | solution.py:179
  31.5 6.9 %collective-permute-start.3 = (bf16[32,512]{1,0:T(8,128)(2,1)S(1)}, bf16[32,512]{1,0:T(8,128)(2,1)S(1)}, u32[]{:S(2)}, u32[]{:S(2)}) collective-permute-start(bf16[32,512]{1,0:T(8,128)(2,1)S(1)} %bitcast.21), channel_id=1, source_target_pairs={{0,2},{1,3},{2,0},{3,1},{4,6},{5,7},{6,4},{7,5},{8,10},{9,11},{10,... | collective-permute-start | bytes 98312 | tf_op jit(solution)/shard_map/ppermute | solution.py:179

commit v3 on v2

--- a/solution.py
+++ b/solution.py
@@ -29,31 +29,43 @@
     return loads
 
 
-def route_kernel(
-    sub_here,
+def fetch_kernel(
+    level_here,
+    pieces_hbm,
     target_hbm,
     subtile_hbm,
     tokens_hbm,
-    bank_ref,
+    half_ref,
     target_ref,
     subtile_ref,
     tokens_ref,
     loaded,
+):
+    far = [target_hbm, subtile_hbm, tokens_hbm]
+    near = [target_ref, subtile_ref, tokens_ref]
+    for i, offset in enumerate(LATER):
+        far.append(pieces_hbm.at[level_here[0] ^ FIRST ^ offset])
+        near.append(half_ref.at[i])
+    for load in start_loads(far, near, loaded):
+        load.wait()
+
+
+def route_kernel(
+    sub_here,
+    target_ref,
+    subtile_ref,
+    tokens_ref,
+    bank_ref,
     *,
     tile_count,
     capacity,
 ):
-    loads = start_loads(
-        (target_hbm, subtile_hbm, tokens_hbm), (target_ref, subtile_ref, tokens_ref), loaded
-    )
     rows = tokens_ref.shape[0]
     width = tokens_ref.shape[1]
     before = lax.broadcasted_iota(jnp.int32, (rows, rows), 0) < lax.broadcasted_iota(
         jnp.int32, (rows, rows), 1
     )
     before = jnp.where(before, 1.0, 0.0).astype(jnp.bfloat16)
-    loads[0].wait()
-    loads[1].wait()
     keep = jnp.abs(subtile_ref[...] - sub_here[0]) <= 1
     target = jnp.where(keep, target_ref[...], -1)
     tile_ids = lax.broadcasted_iota(jnp.int32, (tile_count, rows), 0)
@@ -62,7 +74,6 @@
     rank = jnp.dot(onehot.astype(jnp.bfloat16), before, preferred_element_type=jnp.float32)
     rank = jnp.where(named, rank, -1.0)
     count = jnp.sum(onehot, axis=1, keepdims=True)
-    loads[2].wait()
     tokens = tokens_ref[...]
     group = 8
     slot = lax.broadcasted_iota(jnp.int32, (group, capacity, rows), 1).astype(jnp.float32)
@@ -78,10 +89,6 @@
         ).astype(jnp.bfloat16)
 
 
-def stage_kernel(key_ref, key_columns_ref):
-    key_columns_ref[...] = key_ref[...].astype(jnp.float32).T.astype(jnp.bfloat16)
-
-
 def query_kernel(*refs):
     *piece_refs, weight_ref, columns_ref, query_ref = refs
     columns = jnp.concatenate([ref[...] for ref in piece_refs], axis=0)
@@ -91,22 +98,21 @@
 
 
 def encode_kernel(*refs, block_order):
-    level_here, tokens_ref, key_weight_ref, query_ref, grid_ref = refs[:5]
-    far, encoded_ref, near, loaded = refs[5:12], refs[12], refs[13:20], refs[20]
     (
+        level_here,
+        tokens_ref,
+        key_weight_ref,
         value_weight_ref,
-        sink_ref,
         out_weight_ref,
-        gain_ref,
-        mixing_ref,
-        up_ref,
-        down_ref,
-    ) = near
+        query_ref,
+        grid_ref,
+    ) = refs[:7]
+    far, encoded_ref, near, loaded = refs[7:12], refs[12], refs[13:18], refs[18]
+    sink_ref, gain_ref, mixing_ref, up_ref, down_ref = near
     loads = start_loads(far, near, loaded)
     levels = len(block_order)
     rows, width = query_ref.shape
     head_width = width // HEADS
-    pair = 2 * head_width
     tokens = tokens_ref[...]
     over_tokens = (((1,), (1,)), ((), ()))
     lane = lax.broadcasted_iota(jnp.int32, (16, tokens.shape[1]), 1)
@@ -115,41 +121,42 @@
         first_feature, tokens, over_tokens, preferred_element_type=jnp.float32
     )[0:1]
     bias = jnp.where(marks > EMPTY_FROM, -1e30, 0.0)
-    keys = lax.dot_general(
-        key_weight_ref[...], tokens, over_tokens, preferred_element_type=jnp.float32
-    ).astype(jnp.bfloat16)
-    loads[0].wait()
-    loads[1].wait()
+    keys = jnp.dot(tokens, key_weight_ref[...], preferred_element_type=jnp.float32).astype(
+        jnp.bfloat16
+    )
     values = jnp.dot(tokens, value_weight_ref[...], preferred_element_type=jnp.float32).astype(
         jnp.bfloat16
     )
-    left = lax.broadcasted_iota(jnp.int32, (rows, pair), 1) < head_width
+    group = 2 * head_width
+    lane_head = lax.broadcasted_iota(jnp.int32, (rows, group), 1) // head_width
+    loads[0].wait()
     attended = []
     for p in range(HEADS // 2):
-        lanes = slice(p * pair, (p + 1) * pair)
+        lanes = slice(p * group, (p + 1) * group)
         query = query_ref[:, lanes].astype(jnp.float32) * head_width**-0.5
-        both = jnp.concatenate(
-            [jnp.where(left, query, 0.0), jnp.where(left, 0.0, query)], axis=0
-        ).astype(jnp.bfloat16)
-        scores = jnp.dot(both, keys[lanes], preferred_element_type=jnp.float32) + bias
-        row_head = lax.broadcasted_iota(jnp.int32, (2 * rows, 1), 0) < rows
-        sink = jnp.where(row_head, sink_ref[2 * p], sink_ref[2 * p + 1])
-        peak = jnp.maximum(jnp.max(scores, axis=1, keepdims=True), sink)
-        weights = jnp.exp(scores - peak)
-        total = jnp.exp(sink - peak) + jnp.sum(weights, axis=1, keepdims=True)
-        mixed = jnp.dot(
-            weights.astype(jnp.bfloat16), values[:, lanes], preferred_element_type=jnp.float32
-        )
-        mixed = mixed / total
-        attended.append(jnp.where(left, mixed[:rows], mixed[rows:]).astype(jnp.bfloat16))
+        value = values[:, lanes]
+        value = jnp.concatenate([value, jnp.ones_like(value)], axis=1)
+        mine = None
+        for h in range(2):
+            sink = sink_ref[2 * p + h]
+            one = jnp.where(lane_head == h, query, 0.0).astype(jnp.bfloat16)
+            scores = bias + lax.dot_general(
+                one, keys[:, lanes], over_tokens, preferred_element_type=jnp.float32
+            )
+            peak = jnp.maximum(jnp.max(scores, axis=1, keepdims=True), sink)
+            weights = jnp.exp(scores - peak)
+            mixed = jnp.dot(weights.astype(jnp.bfloat16), value, preferred_element_type=jnp.float32)
+            mixed = mixed[:, :group] / (mixed[:, group:] + jnp.exp(sink - peak))
+            mine = mixed if mine is None else jnp.where(lane_head == h, mixed, mine)
+        attended.append(mine.astype(jnp.bfloat16))
     attended = jnp.concatenate(attended, axis=1)
-    for load in loads[2:5]:
-        load.wait()
     updated = (
         grid_ref[...].astype(jnp.float32)
         + jnp.dot(attended, out_weight_ref[...], preferred_element_type=jnp.float32)
     ).astype(jnp.bfloat16)
     wide = updated.astype(jnp.float32)
+    loads[1].wait()
+    loads[2].wait()
     inverse = lax.rsqrt(jnp.mean(wide * wide, axis=1, keepdims=True) + 1e-05)
     normed = wide * inverse * gain_ref[...]
     cells = rows // levels
@@ -162,11 +169,11 @@
             total = total + mixing_ref[l, held[m]] * parts[m]
         blended.append(total)
     blended = jnp.concatenate(blended, axis=0).astype(jnp.bfloat16)
-    loads[5].wait()
+    loads[3].wait()
     hidden = jax.nn.gelu(
         jnp.dot(blended, up_ref[...], preferred_element_type=jnp.float32)
     ).astype(jnp.bfloat16)
-    loads[6].wait()
+    loads[4].wait()
     encoded = (
         wide + jnp.dot(hidden, down_ref[...], preferred_element_type=jnp.float32)
     ).astype(jnp.bfloat16)
@@ -208,32 +215,42 @@
 
     here = lax.axis_index("lev")
     pieces = grid_state.reshape(levels, cells_here, width)
-    came = exchange_permute(pick(pieces, [here ^ FIRST ^ o for o in LATER]), FIRST, levels)
-    bank = pl.pallas_call(
-        functools.partial(route_kernel, tile_count=tile_count, capacity=capacity),
-        out_shape=jax.ShapeDtypeStruct((tile_count * capacity, token_width), observations.dtype),
-        in_specs=[smem, far, far, far],
-        out_specs=vmem,
-        scratch_shapes=[
+    half, target, subtile_row, tokens = pl.pallas_call(
+        fetch_kernel,
+        out_shape=[
+            pltpu.VMEM((len(LATER), cells_here, width), grid_state.dtype),
             pltpu.VMEM((1, token_rows), jnp.int32),
             pltpu.VMEM((1, token_rows), jnp.int32),
             pltpu.VMEM(observations.shape, observations.dtype),
-            pltpu.SemaphoreType.DMA((3,)),
         ],
-        compiler_params=pltpu.CompilerParams(vmem_limit_bytes=32 * MIB),
-        cost_estimate=pl.CostEstimate(flops=300_000_000, bytes_accessed=MIB, transcendentals=0),
-        name="route",
+        in_specs=[smem] + [far] * 4,
+        out_specs=[vmem] * 4,
+        scratch_shapes=[pltpu.SemaphoreType.DMA((3 + len(LATER),))],
+        compiler_params=pltpu.CompilerParams(vmem_limit_bytes=8 * MIB),
+        cost_estimate=pl.CostEstimate(flops=1000, bytes_accessed=MIB, transcendentals=0),
+        name="fetch",
     )(
-        sub_here,
+        here.reshape(1),
         *(
             pltpu.with_memory_space_constraint(o, pltpu.HBM)
             for o in (
+                pieces,
                 destination.reshape(1, token_rows),
                 subtile.reshape(1, token_rows),
                 observations,
             )
         ),
     )
+    came = exchange_permute(half, FIRST, levels)
+    bank = pl.pallas_call(
+        functools.partial(route_kernel, tile_count=tile_count, capacity=capacity),
+        out_shape=jax.ShapeDtypeStruct((tile_count * capacity, token_width), observations.dtype),
+        in_specs=[smem] + [vmem] * 3,
+        out_specs=vmem,
+        compiler_params=pltpu.CompilerParams(vmem_limit_bytes=32 * MIB),
+        cost_estimate=pl.CostEstimate(flops=300_000_000, bytes_accessed=MIB, transcendentals=0),
+        name="route",
+    )(sub_here, target, subtile_row, tokens)
     bank, came = lax.optimization_barrier((bank, came))
     received = lax.all_to_all(
         bank.reshape(tile_count, capacity, token_width),
@@ -242,15 +259,6 @@
         concat_axis=0,
         tiled=True,
     ).reshape(tile_count * capacity, token_width)
-    key_columns = pl.pallas_call(
-        stage_kernel,
-        out_shape=jax.ShapeDtypeStruct(key_weight.shape[::-1], key_weight.dtype),
-        in_specs=[vmem],
-        out_specs=vmem,
-        compiler_params=pltpu.CompilerParams(vmem_limit_bytes=8 * MIB),
-        cost_estimate=pl.CostEstimate(flops=1000, bytes_accessed=MIB, transcendentals=0),
-        name="stage",
-    )(key_weight)
     parts = []
     for came_block, offset in zip(came, LATER):
         both = jnp.stack([pick(pieces, [here ^ offset])[0], came_block])
@@ -266,9 +274,7 @@
         name="query",
     )(*parts, query_weight)
     operands = [
-        value_weight,
         sink_logit,
-        out_weight,
         norm_gain.reshape(1, width),
         mixing,
         up_weight,
@@ -280,7 +286,7 @@
             encode_kernel, block_order=[o ^ first for o in LATER for first in (0, FIRST)]
         ),
         out_shape=jax.ShapeDtypeStruct((rows, width), jnp.bfloat16),
-        in_specs=[smem] + [vmem] * 4 + [far] * len(operands),
+        in_specs=[smem] + [vmem] * 6 + [far] * len(operands),
         out_specs=vmem,
         scratch_shapes=[
             (pltpu.SMEM if operand.shape[-1] == HEADS else pltpu.VMEM)(operand.shape, operand.dtype)
@@ -292,7 +298,7 @@
             flops=1_500_000_000, bytes_accessed=5 * MIB, transcendentals=1_200_000
         ),
         name="encode",
-    )(here.reshape(1), received, key_columns, queries, columns, *operands)
+    )(here.reshape(1), received, key_weight, value_weight, out_weight, queries, columns, *operands)
     return lax.all_to_all(
         encoded.reshape(levels, cells_here, width), "lev", split_axis=0, concat_axis=1, tiled=True
     )

time: 60.9 us -> 59.5 us (0.977)
  Pallas kernels: 7.72 us -> 6.35 us
  waiting for transfers between devices: 5.05 us -> 5.9 us
  local copies, waits for them, and re-layouts: 1.52 us -> 0.7 us
    pallas_call x1, Pallas kernels: 5.08 us -> 3.64 us  [body(): pl.pallas_call(functools.partial(encode_kernel, block_order=[o ^ first fo...]
    pallas_call x1, Pallas kernels: 0.14 us -> 1.05 us  [body(): pl.pallas_call(fetch_kernel, out_shape=[pltpu.VMEM((len(LATER), cells_her...]
    ppermute x4, waiting for transfers between devices: 5.05 us -> 5.89 us  [exchange_permute(): return lax.ppermute(array, 'lev', [(i, i ^ offset) for i in range(count)])]
    pallas_call x1, Pallas kernels: 2.27 us -> 1.43 us  [body(): pl.pallas_call(functools.partial(route_kernel, tile_count=tile_count, cap...]
    dynamic_slice x1, local copies, waits for them, and re-layouts: 0.85 us -> 0.01 us  [pick(): lax.dynamic_index_in_dim(pieces, l, 0, keepdims=False)]
  transfers between devices with their start and end apart: 5 -> 5, of which waited for: 3 -> 3; matrix products, arithmetic and copies ran while one was open for 0% -> 0% of each run, Pallas kernels for 4% -> 3%
where the time goes in v3:
time: 59.5 us; the launch traced here: 59.2 us
  starting transfers between devices  30.1 us (51%)
  blocking collectives  15.9 us (27%)
  Pallas kernels  6.35 us (11%)
  waiting for transfers between devices  5.9 us (10%)
  local copies, waits for them, and re-layouts  0.7 us (1%)
    ppermute x4, starting transfers between devices, exchange_permute(): return lax.ppermute(array, 'lev', [(i, i ^ offset) for i in range(count)])  16 us
    all_to_all x1, blocking collectives, body(): lax.all_to_all(encoded.reshape(levels, cells_here, width), 'lev', split_a...  15.9 us
    all_to_all x1, starting transfers between devices, body(): lax.all_to_all(bank.reshape(tile_count, capacity, token_width), 'tile', s...  14.2 us
    ppermute x4, waiting for transfers between devices, exchange_permute(): return lax.ppermute(array, 'lev', [(i, i ^ offset) for i in range(count)])  5.89 us
    pallas_call x1, Pallas kernels, body(): pl.pallas_call(functools.partial(encode_kernel, block_order=[o ^ first fo...  3.64 us
    pallas_call x1, Pallas kernels, body(): pl.pallas_call(functools.partial(route_kernel, tile_count=tile_count, cap...  1.43 us
  transfers between devices with their start and end apart: 5, of which 3 were waited for; matrix products, arithmetic and copies ran while one was open for 0% of the time, Pallas kernels for 3%

profile of v3, /device:TPU:6, one launch (start us, length us, event | category | flops | bytes accessed | tf_op | source)
XLA Modules:
  0.0 59.2 jit_solution(3436405778367617110)
XLA Ops:
  0.0 1.0 %fetch.1 = (bf16[4,16,512]{2,1,0:T(8,128)(2,1)S(1)}, s32[1,512]{1,0:T(1,128)S(1)}, s32[1,512]{1,0:T(1,128)S(1)}, bf16[512,256]{1,0:T(8,128)(2,1)S(1)}) custom-call(s32[1]{0:T(128)} %bitcast.level_here.refs_0_, bf16[8,16,512]{2,1,0:T(8,128)(2,1)} %bitcast.18, s32[1,512]{1,0:T(1,128)} %bitcast.23, s32[1,512]{1,0:T(1,128)} %bitcast.24, bf16[512,256]{1,0:T(8,128)(2,1)} %tokens_hbm.1), custom_call_target="tpu_custom_call" | custom-call | flops 1000 | bytes 1048576 | tf_op jit(solution)/shard_map/fetch/pallas_call | solution.py:218
  1.1 3.5 %collective-permute-start = (bf16[4,16,512]{2,1,0:T(8,128)(2,1)S(1)}, bf16[4,16,512]{2,1,0:T(8,128)(2,1)S(1)}, u32[]{:S(2)}, u32[]{:S(2)}) collective-permute-start(bf16[4,16,512]{2,1,0:T(8,128)(2,1)S(1)} %get-tuple-element.16), channel_id=1, source_target_pairs={{0,1},{1,0},{2,3},{3,2},{4,5},{5,4},{6,7},{7,6},{8,9},{9,8},{10,11... | collective-permute-start | bytes 196616 | tf_op jit(solution)/shard_map/ppermute | solution.py:186
  4.6 1.4 %route.1 = bf16[1024,256]{1,0:T(8,128)(2,1)} custom-call(s32[1]{0:T(128)} %bitcast.1.sub_here, s32[1,512]{1,0:T(1,128)S(1)} %get-tuple-element.13.target_ref, s32[1,512]{1,0:T(1,128)S(1)} %get-tuple-element.14.subtile_ref, bf16[512,256]{1,0:T(8,128)(2,1)S(1)} %get-tuple-element.15.tokens_ref), custom_call_target="tpu_custom_call" | custom-call | flops 300000000 | bytes 1048576 | tf_op jit(solution)/shard_map/route/pallas_call | solution.py:245
  6.0 1.2 %collective-permute-done = bf16[4,16,512]{2,1,0:T(8,128)(2,1)S(1)} collective-permute-done((bf16[4,16,512]{2,1,0:T(8,128)(2,1)S(1)}, bf16[4,16,512]{2,1,0:T(8,128)(2,1)S(1)}, u32[]{:S(2)}, u32[]{:S(2)}) %collective-permute-start) | collective-permute-done | bytes 65568 | tf_op jit(solution)/shard_map/ppermute | solution.py:186
  7.2 0.0 copy-start.4
  7.2 0.0 copy-start.2
  7.2 0.0 copy-start.3
  7.2 14.2 %all-to-all-start = ((bf16[64,16,256]{2,1,0:T(8,128)(2,1)}), bf16[64,16,256]{2,1,0:T(8,128)(2,1)S(1)}, u32[]{:S(2)}, u32[]{:S(2)}) async-start(bf16[64,16,256]{2,1,0:T(8,128)(2,1)} %bitcast.5), calls=%async_computation | async-start | bytes 1048576 | tf_op jit(solution)/shard_map/all_to_all | solution.py:255
  21.4 0.0 copy-start
  21.4 0.0 copy-done.4
  21.4 0.0 copy-start.1
  21.5 7.1 %collective-permute-start.1 = (bf16[32,512]{1,0:T(8,128)(2,1)S(1)}, bf16[32,512]{1,0:T(8,128)(2,1)S(1)}, u32[]{:S(2)}, u32[]{:S(2)}) collective-permute-start(bf16[32,512]{1,0:T(8,128)(2,1)S(1)} %bitcast.20), channel_id=1, source_target_pairs={{0,5},{1,4},{2,7},{3,6},{4,1},{5,0},{6,3},{7,2},{8,13},{9,12},{10,... | collective-permute-start | bytes 98312 | tf_op jit(solution)/shard_map/ppermute | solution.py:186
  28.6 3.1 %collective-permute-start.2 = (bf16[32,512]{1,0:T(8,128)(2,1)S(1)}, bf16[32,512]{1,0:T(8,128)(2,1)S(1)}, u32[]{:S(2)}, u32[]{:S(2)}) collective-permute-start(bf16[32,512]{1,0:T(8,128)(2,1)S(1)} %bitcast.21), channel_id=1, source_target_pairs={{0,6},{1,7},{2,4},{3,5},{4,2},{5,3},{6,0},{7,1},{8,14},{9,15},{10,... | collective-permute-start | bytes 98312 | tf_op jit(solution)/shard_map/ppermute | solution.py:186
  31.8 2.2 %collective-permute-start.3 = (bf16[32,512]{1,0:T(8,128)(2,1)S(1)}, bf16[32,512]{1,0:T(8,128)(2,1)S(1)}, u32[]{:S(2)}, u32[]{:S(2)}) collective-permute-start(bf16[32,512]{1,0:T(8,128)(2,1)S(1)} %bitcast.22), channel_id=1, source_target_pairs={{0,2},{1,3},{2,0},{3,1},{4,6},{5,7},{6,4},{7,5},{8,10},{9,11},{10,... | collective-permute-start | bytes 98312 | tf_op jit(solution)/shard_map/ppermute | solution.py:186
  34.0 0.0 collective-permute-done.1.refs_1_
  34.0 2.5 %collective-permute-done.2.refs_2_ = bf16[32,512]{1,0:T(8,128)(2,1)S(1)} collective-permute-done((bf16[32,512]{1,0:T(8,128)(2,1)S(1)}, bf16[32,512]{1,0:T(8,128)(2,1)S(1)}, u32[]{:S(2)}, u32[]{:S(2)}) %collective-permute-start.2) | collective-permute-done | bytes 32800 | tf_op jit(solution)/shard_map/ppermute | solution.py:186
  36.5 2.2 %collective-permute-done.3.refs_3_ = bf16[32,512]{1,0:T(8,128)(2,1)S(1)} collective-permute-done((bf16[32,512]{1,0:T(8,128)(2,1)S(1)}, bf16[32,512]{1,0:T(8,128)(2,1)S(1)}, u32[]{:S(2)}, u32[]{:S(2)}) %collective-permute-start.3) | collective-permute-done | bytes 32800 | tf_op jit(solution)/shard_map/ppermute | solution.py:186
  38.7 0.0 copy-done
  38.7 0.2 query.1
  38.9 0.0 all-to-all-done
  38.9 0.0 copy-done.2
  39.0 0.0 copy-done.3
  39.0 0.0 copy-done.1
  39.0 3.6 %encode.1 = bf16[128,512]{1,0:T(8,128)(2,1)S(1)} custom-call(s32[1]{0:T(128)} %bitcast.level_here.refs_0_, bf16[1024,256]{1,0:T(8,128)(2,1)S(1)} %bitcast.14, bf16[256,512]{1,0:T(8,128)(2,1)S(1)} %copy-done.2, bf16[256,512]{1,0:T(8,128)(2,1)S(1)} %copy-done.3, bf16[512,512]{1,0:T(8,128)(2,1)S(1)} %copy-done.1, ...), custom_call_target="tpu_custom_call" | custom-call | flops 1500000000 | bytes 5242880 | tf_op jit(solution)/shard_map/encode/pallas_call | solution.py:284
  42.6 15.9 %all_to_all.17 = bf16[8,16,512]{2,1,0:T(8,128)(2,1)S(1)} all-to-all(bf16[8,16,512]{2,1,0:T(8,128)(2,1)S(1)} %bitcast.16), channel_id=1, replica_groups=mesh['tile'=64,'lev'=8] {'lev'}, dimensions={0} | all-to-all | bytes 262144 | tf_op jit(solution)/shard_map/all_to_all | solution.py:302
  58.5 0.7 %copy.15 = bf16[1,128,512]{2,1,0:T(8,128)(2,1)} copy(bf16[1,128,512]{2,1,0:T(8,128)(2,1)S(1)} %bitcast.17) | data formatting | bytes 262144
  (6 shorter events, 0.0 us)
Async XLA Ops:
  1.1 6.2 %collective-permute-start = (bf16[4,16,512]{2,1,0:T(8,128)(2,1)S(1)}, bf16[4,16,512]{2,1,0:T(8,128)(2,1)S(1)}, u32[]{:S(2)}, u32[]{:S(2)}) collective-permute-start(bf16[4,16,512]{2,1,0:T(8,128)(2,1)S(1)} %get-tuple-element.16), channel_id=1, source_target_pairs={{0,1},{1,0},{2,3},{3,2},{4,5},{5,4},{6,7},{7,6},{8,9},{9,8},{10,11... | collective-permute-start | bytes 196616 | tf_op jit(solution)/shard_map/ppermute | solution.py:186
  7.2 14.2 %copy-start.4 = (bf16[1,128,512]{2,1,0:T(8,128)(2,1)S(1)}, bf16[1,128,512]{2,1,0:T(8,128)(2,1)}, u32[]{:S(2)}) copy-start(bf16[1,128,512]{2,1,0:T(8,128)(2,1)} %param.13) | copy-start | bytes 393220
  7.2 31.7 %copy-start.2 = (bf16[256,512]{1,0:T(8,128)(2,1)S(1)}, bf16[256,512]{1,0:T(8,128)(2,1)}, u32[]{:S(2)}) copy-start(bf16[256,512]{1,0:T(8,128)(2,1)} %refs_2_.1) | copy-start | bytes 786436
  7.2 31.7 %copy-start.3 = (bf16[256,512]{1,0:T(8,128)(2,1)S(1)}, bf16[256,512]{1,0:T(8,128)(2,1)}, u32[]{:S(2)}) copy-start(bf16[256,512]{1,0:T(8,128)(2,1)} %refs_3_.1) | copy-start | bytes 786436
  7.2 31.7 %all-to-all-start = ((bf16[64,16,256]{2,1,0:T(8,128)(2,1)}), bf16[64,16,256]{2,1,0:T(8,128)(2,1)S(1)}, u32[]{:S(2)}, u32[]{:S(2)}) async-start(bf16[64,16,256]{2,1,0:T(8,128)(2,1)} %bitcast.5), calls=%async_computation | async-start | bytes 1048576 | tf_op jit(solution)/shard_map/all_to_all | solution.py:255
  21.4 17.3 %copy-start = (bf16[512,512]{1,0:T(8,128)(2,1)S(1)}, bf16[512,512]{1,0:T(8,128)(2,1)}, u32[]{:S(2)}) copy-start(bf16[512,512]{1,0:T(8,128)(2,1)} %refs_4_.2) | copy-start | bytes 1572868
  21.4 17.5 %copy-start.1 = (bf16[512,512]{1,0:T(8,128)(2,1)S(1)}, bf16[512,512]{1,0:T(8,128)(2,1)}, u32[]{:S(2)}) copy-start(bf16[512,512]{1,0:T(8,128)(2,1)} %refs_4_.3) | copy-start | bytes 1572868
  21.5 12.5 %collective-permute-start.1 = (bf16[32,512]{1,0:T(8,128)(2,1)S(1)}, bf16[32,512]{1,0:T(8,128)(2,1)S(1)}, u32[]{:S(2)}, u32[]{:S(2)}) collective-permute-start(bf16[32,512]{1,0:T(8,128)(2,1)S(1)} %bitcast.20), channel_id=1, source_target_pairs={{0,5},{1,4},{2,7},{3,6},{4,1},{5,0},{6,3},{7,2},{8,13},{9,12},{10,... | collective-permute-start | bytes 98312 | tf_op jit(solution)/shard_map/ppermute | solution.py:186
  28.6 7.9 %collective-permute-start.2 = (bf16[32,512]{1,0:T(8,128)(2,1)S(1)}, bf16[32,512]{1,0:T(8,128)(2,1)S(1)}, u32[]{:S(2)}, u32[]{:S(2)}) collective-permute-start(bf16[32,512]{1,0:T(8,128)(2,1)S(1)} %bitcast.21), channel_id=1, source_target_pairs={{0,6},{1,7},{2,4},{3,5},{4,2},{5,3},{6,0},{7,1},{8,14},{9,15},{10,... | collective-permute-start | bytes 98312 | tf_op jit(solution)/shard_map/ppermute | solution.py:186
  31.8 6.9 %collective-permute-start.3 = (bf16[32,512]{1,0:T(8,128)(2,1)S(1)}, bf16[32,512]{1,0:T(8,128)(2,1)S(1)}, u32[]{:S(2)}, u32[]{:S(2)}) collective-permute-start(bf16[32,512]{1,0:T(8,128)(2,1)S(1)} %bitcast.22), channel_id=1, source_target_pairs={{0,2},{1,3},{2,0},{3,1},{4,6},{5,7},{6,4},{7,5},{8,10},{9,11},{10,... | collective-permute-start | bytes 98312 | tf_op jit(solution)/shard_map/ppermute | solution.py:186

commit v4 on v3

--- a/solution.py
+++ b/solution.py
@@ -15,7 +15,7 @@
 
 
 FIRST = 1
-LATER = (0, 5, 6, 2)
+LATER = (0, 2, 6, 5)
 
 
 def pick(pieces, levels):
@@ -56,10 +56,12 @@
     subtile_ref,
     tokens_ref,
     bank_ref,
-    *,
+    *spare_ref,
     tile_count,
     capacity,
 ):
+    for ref in spare_ref:
+        ref[...] = jnp.zeros(ref.shape, ref.dtype)
     rows = tokens_ref.shape[0]
     width = tokens_ref.shape[1]
     before = lax.broadcasted_iota(jnp.int32, (rows, rows), 0) < lax.broadcasted_iota(
@@ -241,16 +243,33 @@
             )
         ),
     )
-    came = exchange_permute(half, FIRST, levels)
-    bank = pl.pallas_call(
-        functools.partial(route_kernel, tile_count=tile_count, capacity=capacity),
-        out_shape=jax.ShapeDtypeStruct((tile_count * capacity, token_width), observations.dtype),
-        in_specs=[smem] + [vmem] * 3,
-        out_specs=vmem,
-        compiler_params=pltpu.CompilerParams(vmem_limit_bytes=32 * MIB),
-        cost_estimate=pl.CostEstimate(flops=300_000_000, bytes_accessed=MIB, transcendentals=0),
-        name="route",
-    )(sub_here, target, subtile_row, tokens)
+    bank_shape = jax.ShapeDtypeStruct((tile_count * capacity, token_width), observations.dtype)
+    half_shape = jax.ShapeDtypeStruct(half.shape, half.dtype)
+
+    def route(out_shape):
+        return pl.pallas_call(
+            functools.partial(route_kernel, tile_count=tile_count, capacity=capacity),
+            out_shape=out_shape,
+            in_specs=[smem] + [vmem] * 3,
+            out_specs=[vmem] * len(out_shape),
+            compiler_params=pltpu.CompilerParams(vmem_limit_bytes=32 * MIB),
+            cost_estimate=pl.CostEstimate(
+                flops=300_000_000, bytes_accessed=MIB, transcendentals=0
+            ),
+            name="route",
+        )
+
+    early = (lax.axis_index("tile") // 2) % 8 < 3
+    bank, came = lax.cond(
+        early,
+        lambda h, *of: (route([bank_shape])(*of)[0], exchange_permute(h, FIRST, levels)),
+        lambda h, *of: tuple(route([bank_shape, half_shape])(*of)),
+        half,
+        sub_here,
+        target,
+        subtile_row,
+        tokens,
+    )
     bank, came = lax.optimization_barrier((bank, came))
     received = lax.all_to_all(
         bank.reshape(tile_count, capacity, token_width),
@@ -259,6 +278,10 @@
         concat_axis=0,
         tiled=True,
     ).reshape(tile_count * capacity, token_width)
+    came_late = lax.cond(
+        early, jnp.zeros_like, lambda h: exchange_permute(h, FIRST, levels), half
+    )
+    came = jnp.where(early, came, came_late)
     parts = []
     for came_block, offset in zip(came, LATER):
         both = jnp.stack([pick(pieces, [here ^ offset])[0], came_block])

time: 59.5 us -> 56.3 us (0.946)
  the two profiles are of different devices: /device:TPU:6 before, /device:TPU:198 now
where the time goes in v4:
time: 56.3 us; the launch traced here: 55.9 us
  starting transfers between devices  26.5 us (47%)
  blocking collectives  13.1 us (23%)
  waiting for transfers between devices  8.38 us (15%)
  Pallas kernels  6.34 us (11%)
  local copies, waits for them, and re-layouts  1.38 us (2%)
    ppermute x4, starting transfers between devices, exchange_permute(): return lax.ppermute(array, 'lev', [(i, i ^ offset) for i in range(count)])  14 us
    all_to_all x1, blocking collectives, body(): lax.all_to_all(encoded.reshape(levels, cells_here, width), 'lev', split_a...  13.1 us
    all_to_all x1, starting transfers between devices, body(): lax.all_to_all(bank.reshape(tile_count, capacity, token_width), 'tile', s...  12.5 us
    ppermute x4, waiting for transfers between devices, exchange_permute(): return lax.ppermute(array, 'lev', [(i, i ^ offset) for i in range(count)])  8.38 us
    pallas_call x1, Pallas kernels, body(): pl.pallas_call(functools.partial(encode_kernel, block_order=[o ^ first fo...  3.64 us
    pallas_call x1, Pallas kernels, body(): route([bank_shape, half_shape])(*of)  1.43 us
    unnamed x11, local copies, waits for them, and re-layouts  1.36 us
  transfers between devices with their start and end apart: 5, of which 3 were waited for; matrix products, arithmetic and copies ran while one was open for 0% of the time, Pallas kernels for 0%

profile of v4, /device:TPU:198, one launch (start us, length us, event | category | flops | bytes accessed | tf_op | source)
XLA Modules:
  0.0 55.9 jit_solution(2244435674463505973)
XLA Ops:
  0.0 1.0 %fetch.1 = (bf16[4,16,512]{2,1,0:T(8,128)(2,1)S(1)}, s32[1,512]{1,0:T(1,128)S(1)}, s32[1,512]{1,0:T(1,128)S(1)}, bf16[512,256]{1,0:T(8,128)(2,1)S(1)}) custom-call(s32[1]{0:T(128)} %bitcast.level_here.refs_0_, bf16[8,16,512]{2,1,0:T(8,128)(2,1)} %bitcast.18, s32[1,512]{1,0:T(1,128)} %bitcast.23, s32[1,512]{1,0:T(1,128)} %bitcast.24, bf16[512,256]{1,0:T(8,128)(2,1)} %tokens_hbm.1), custom_call_target="tpu_custom_call" | custom-call | flops 1000 | bytes 1048576 | tf_op jit(solution)/shard_map/fetch/pallas_call | solution.py:220
  1.1 1.4 %conditional.2 = ((bf16[1024,256]{1,0:T(8,128)(2,1)}, bf16[4,16,512]{2,1,0:T(8,128)(2,1)})) conditional(s32[]{:T(128)} %convert_element_type.4, (s32[1]{0:T(128)}, s32[1,512]{1,0:T(1,128)S(1)}, s32[1,512]{1,0:T(1,128)S(1)}, bf16[512,256]{1,0:T(8,128)(2,1)S(1)}) %tuple.18, (s32[1]{0:T(128)}, s32[1,512]{1,0:T(1,128)S(1)}, s32[1,512]{1,0:T(1,128)S(1)}, ...), branch_computations={%region_0.1_spmd, %region_1.2_spmd} | conditional | flops 300000000 | bytes 1310784 | solution.py:263
  1.1 1.4 %route.2 = (bf16[1024,256]{1,0:T(8,128)(2,1)}, bf16[4,16,512]{2,1,0:T(8,128)(2,1)}) custom-call(s32[1]{0:T(128)} %get-tuple-element.27.sub_here, s32[1,512]{1,0:T(1,128)S(1)} %get-tuple-element.28.target_ref, s32[1,512]{1,0:T(1,128)S(1)} %get-tuple-element.29.subtile_ref, bf16[512,256]{1,0:T(8,128)(2,1)S(1)} %get-tuple-element.30.tokens_ref), custom_call_target="tpu_custom_call" | custom-call | flops 300000000 | bytes 1048576 | tf_op jit(solution)/shard_map/cond/branch_0_fun/route/pallas_call | solution.py:266
  2.5 0.0 copy-start.4
  2.5 0.0 copy-start.3
  2.5 12.5 %all-to-all-start = ((bf16[64,16,256]{2,1,0:T(8,128)(2,1)}), bf16[64,16,256]{2,1,0:T(8,128)(2,1)S(1)}, u32[]{:S(2)}, u32[]{:S(2)}) async-start(bf16[64,16,256]{2,1,0:T(8,128)(2,1)} %bitcast.5), calls=%async_computation | async-start | bytes 1048576 | tf_op jit(solution)/shard_map/all_to_all | solution.py:274
  15.1 0.0 copy-start
  15.1 6.3 %conditional.3 = (bf16[4,16,512]{2,1,0:T(8,128)(2,1)S(1)}) conditional(s32[]{:T(128)} %convert_element_type.4, bf16[4,16,512]{2,1,0:T(8,128)(2,1)S(1)} %get-tuple-element.47, () %tuple.20), branch_computations={%region_2.3_spmd, %region_3.4_spmd} | conditional | bytes 262192 | solution.py:281
  15.1 2.6 %collective-permute-start.1 = (bf16[4,16,512]{2,1,0:T(8,128)(2,1)S(1)}, bf16[4,16,512]{2,1,0:T(8,128)(2,1)S(1)}, u32[]{:S(2)}, u32[]{:S(2)}) collective-permute-start(bf16[4,16,512]{2,1,0:T(8,128)(2,1)S(1)} %param.2), channel_id=1, source_target_pairs={{0,1},{1,0},{2,3},{3,2},{4,5},{5,4},{6,7},{7,6},{8,9},{9,8},{10,11... | collective-permute-start | bytes 196616 | tf_op jit(solution)/shard_map/cond/branch_0_fun/ppermute | solution.py:188
  17.7 3.7 %collective-permute-done.1 = bf16[4,16,512]{2,1,0:T(8,128)(2,1)S(1)} collective-permute-done((bf16[4,16,512]{2,1,0:T(8,128)(2,1)S(1)}, bf16[4,16,512]{2,1,0:T(8,128)(2,1)S(1)}, u32[]{:S(2)}, u32[]{:S(2)}) %collective-permute-start.1) | collective-permute-done | bytes 65568 | tf_op jit(solution)/shard_map/cond/branch_0_fun/ppermute | solution.py:188
  21.4 0.0 copy-done.4
  21.4 0.0 copy-start.1
  21.5 6.0 %collective-permute-start.4 = (bf16[32,512]{1,0:T(8,128)(2,1)S(1)}, bf16[32,512]{1,0:T(8,128)(2,1)S(1)}, u32[]{:S(2)}, u32[]{:S(2)}) collective-permute-start(bf16[32,512]{1,0:T(8,128)(2,1)S(1)} %bitcast.20), channel_id=1, source_target_pairs={{0,5},{1,4},{2,7},{3,6},{4,1},{5,0},{6,3},{7,2},{8,13},{9,12},{10,... | collective-permute-start | bytes 98312 | tf_op jit(solution)/shard_map/ppermute | solution.py:188
  27.5 3.1 %collective-permute-start.3 = (bf16[32,512]{1,0:T(8,128)(2,1)S(1)}, bf16[32,512]{1,0:T(8,128)(2,1)S(1)}, u32[]{:S(2)}, u32[]{:S(2)}) collective-permute-start(bf16[32,512]{1,0:T(8,128)(2,1)S(1)} %bitcast.21), channel_id=1, source_target_pairs={{0,6},{1,7},{2,4},{3,5},{4,2},{5,3},{6,0},{7,1},{8,14},{9,15},{10,... | collective-permute-start | bytes 98312 | tf_op jit(solution)/shard_map/ppermute | solution.py:188
  30.7 2.3 %collective-permute-start.2 = (bf16[32,512]{1,0:T(8,128)(2,1)S(1)}, bf16[32,512]{1,0:T(8,128)(2,1)S(1)}, u32[]{:S(2)}, u32[]{:S(2)}) collective-permute-start(bf16[32,512]{1,0:T(8,128)(2,1)S(1)} %bitcast.22), channel_id=1, source_target_pairs={{0,2},{1,3},{2,0},{3,1},{4,6},{5,7},{6,4},{7,5},{8,10},{9,11},{10,... | collective-permute-start | bytes 98312 | tf_op jit(solution)/shard_map/ppermute | solution.py:188
  32.9 0.0 collective-permute-done.4.refs_3_
  33.0 2.6 %collective-permute-done.3.refs_2_ = bf16[32,512]{1,0:T(8,128)(2,1)S(1)} collective-permute-done((bf16[32,512]{1,0:T(8,128)(2,1)S(1)}, bf16[32,512]{1,0:T(8,128)(2,1)S(1)}, u32[]{:S(2)}, u32[]{:S(2)}) %collective-permute-start.3) | collective-permute-done | bytes 32800 | tf_op jit(solution)/shard_map/ppermute | solution.py:188
  35.5 2.1 %collective-permute-done.2.refs_1_ = bf16[32,512]{1,0:T(8,128)(2,1)S(1)} collective-permute-done((bf16[32,512]{1,0:T(8,128)(2,1)S(1)}, bf16[32,512]{1,0:T(8,128)(2,1)S(1)}, u32[]{:S(2)}, u32[]{:S(2)}) %collective-permute-start.2) | collective-permute-done | bytes 32800 | tf_op jit(solution)/shard_map/ppermute | solution.py:188
  37.6 0.0 copy-done
  37.6 0.0 copy-start.2
  37.6 0.2 query.1
  37.9 0.0 all-to-all-done
  37.9 0.0 copy-done.3
  37.9 0.0 copy-done.1
  37.9 0.7 %copy-done.2 = bf16[256,512]{1,0:T(8,128)(2,1)S(1)} copy-done((bf16[256,512]{1,0:T(8,128)(2,1)S(1)}, bf16[256,512]{1,0:T(8,128)(2,1)}, u32[]{:S(2)}) %copy-start.2) | copy-done | bytes 262168
  38.6 3.6 %encode.1 = bf16[128,512]{1,0:T(8,128)(2,1)S(1)} custom-call(s32[1]{0:T(128)} %bitcast.level_here.refs_0_, bf16[1024,256]{1,0:T(8,128)(2,1)S(1)} %bitcast.14, bf16[256,512]{1,0:T(8,128)(2,1)S(1)} %copy-done.2, bf16[256,512]{1,0:T(8,128)(2,1)S(1)} %copy-done.3, bf16[512,512]{1,0:T(8,128)(2,1)S(1)} %copy-done.1, ...), custom_call_target="tpu_custom_call" | custom-call | flops 1500000000 | bytes 5242880 | tf_op jit(solution)/shard_map/encode/pallas_call | solution.py:307
  42.2 13.1 %all_to_all.17 = bf16[8,16,512]{2,1,0:T(8,128)(2,1)S(1)} all-to-all(bf16[8,16,512]{2,1,0:T(8,128)(2,1)S(1)} %bitcast.16), channel_id=1, replica_groups=mesh['tile'=64,'lev'=8] {'lev'}, dimensions={0} | all-to-all | bytes 262144 | tf_op jit(solution)/shard_map/all_to_all | solution.py:325
  55.3 0.7 %copy.21 = bf16[1,128,512]{2,1,0:T(8,128)(2,1)} copy(bf16[1,128,512]{2,1,0:T(8,128)(2,1)S(1)} %bitcast.17) | data formatting | bytes 262144
  (6 shorter events, 0.1 us)
Async XLA Ops:
  2.5 18.9 %copy-start.4 = (bf16[1,128,512]{2,1,0:T(8,128)(2,1)S(1)}, bf16[1,128,512]{2,1,0:T(8,128)(2,1)}, u32[]{:S(2)}) copy-start(bf16[1,128,512]{2,1,0:T(8,128)(2,1)} %param.17) | copy-start | bytes 393220
  2.5 35.4 %copy-start.3 = (bf16[256,512]{1,0:T(8,128)(2,1)S(1)}, bf16[256,512]{1,0:T(8,128)(2,1)}, u32[]{:S(2)}) copy-start(bf16[256,512]{1,0:T(8,128)(2,1)} %refs_3_.1) | copy-start | bytes 786436
  2.5 35.3 %all-to-all-start = ((bf16[64,16,256]{2,1,0:T(8,128)(2,1)}), bf16[64,16,256]{2,1,0:T(8,128)(2,1)S(1)}, u32[]{:S(2)}, u32[]{:S(2)}) async-start(bf16[64,16,256]{2,1,0:T(8,128)(2,1)} %bitcast.5), calls=%async_computation | async-start | bytes 1048576 | tf_op jit(solution)/shard_map/all_to_all | solution.py:274
  15.1 22.6 %copy-start = (bf16[512,512]{1,0:T(8,128)(2,1)S(1)}, bf16[512,512]{1,0:T(8,128)(2,1)}, u32[]{:S(2)}) copy-start(bf16[512,512]{1,0:T(8,128)(2,1)} %refs_4_.2) | copy-start | bytes 1572868
  15.1 6.3 %collective-permute-start.1 = (bf16[4,16,512]{2,1,0:T(8,128)(2,1)S(1)}, bf16[4,16,512]{2,1,0:T(8,128)(2,1)S(1)}, u32[]{:S(2)}, u32[]{:S(2)}) collective-permute-start(bf16[4,16,512]{2,1,0:T(8,128)(2,1)S(1)} %param.2), channel_id=1, source_target_pairs={{0,1},{1,0},{2,3},{3,2},{4,5},{5,4},{6,7},{7,6},{8,9},{9,8},{10,11... | collective-permute-start | bytes 196616 | tf_op jit(solution)/shard_map/cond/branch_0_fun/ppermute | solution.py:188
  21.4 16.4 %copy-start.1 = (bf16[512,512]{1,0:T(8,128)(2,1)S(1)}, bf16[512,512]{1,0:T(8,128)(2,1)}, u32[]{:S(2)}) copy-start(bf16[512,512]{1,0:T(8,128)(2,1)} %refs_4_.3) | copy-start | bytes 1572868
  21.5 11.5 %collective-permute-start.4 = (bf16[32,512]{1,0:T(8,128)(2,1)S(1)}, bf16[32,512]{1,0:T(8,128)(2,1)S(1)}, u32[]{:S(2)}, u32[]{:S(2)}) collective-permute-start(bf16[32,512]{1,0:T(8,128)(2,1)S(1)} %bitcast.20), channel_id=1, source_target_pairs={{0,5},{1,4},{2,7},{3,6},{4,1},{5,0},{6,3},{7,2},{8,13},{9,12},{10,... | collective-permute-start | bytes 98312 | tf_op jit(solution)/shard_map/ppermute | solution.py:188
  27.5 8.0 %collective-permute-start.3 = (bf16[32,512]{1,0:T(8,128)(2,1)S(1)}, bf16[32,512]{1,0:T(8,128)(2,1)S(1)}, u32[]{:S(2)}, u32[]{:S(2)}) collective-permute-start(bf16[32,512]{1,0:T(8,128)(2,1)S(1)} %bitcast.21), channel_id=1, source_target_pairs={{0,6},{1,7},{2,4},{3,5},{4,2},{5,3},{6,0},{7,1},{8,14},{9,15},{10,... | collective-permute-start | bytes 98312 | tf_op jit(solution)/shard_map/ppermute | solution.py:188
  30.7 6.9 %collective-permute-start.2 = (bf16[32,512]{1,0:T(8,128)(2,1)S(1)}, bf16[32,512]{1,0:T(8,128)(2,1)S(1)}, u32[]{:S(2)}, u32[]{:S(2)}) collective-permute-start(bf16[32,512]{1,0:T(8,128)(2,1)S(1)} %bitcast.22), channel_id=1, source_target_pairs={{0,2},{1,3},{2,0},{3,1},{4,6},{5,7},{6,4},{7,5},{8,10},{9,11},{10,... | collective-permute-start | bytes 98312 | tf_op jit(solution)/shard_map/ppermute | solution.py:188
  37.6 1.0 %copy-start.2 = (bf16[256,512]{1,0:T(8,128)(2,1)S(1)}, bf16[256,512]{1,0:T(8,128)(2,1)}, u32[]{:S(2)}) copy-start(bf16[256,512]{1,0:T(8,128)(2,1)} %refs_2_.1) | copy-start | bytes 786436

commit v5 on v4

--- a/solution.py
+++ b/solution.py
@@ -92,7 +92,7 @@
 
 
 def query_kernel(*refs):
-    *piece_refs, weight_ref, columns_ref, query_ref = refs
+    *piece_refs, weight_ref, _, _, _, columns_ref, query_ref = refs
     columns = jnp.concatenate([ref[...] for ref in piece_refs], axis=0)
     columns_ref[...] = columns
     query = jnp.dot(columns, weight_ref[...], preferred_element_type=jnp.float32)
@@ -290,12 +290,12 @@
     columns, queries = pl.pallas_call(
         query_kernel,
         out_shape=[jax.ShapeDtypeStruct((rows, width), jnp.bfloat16)] * 2,
-        in_specs=[vmem] * (len(parts) + 1),
+        in_specs=[vmem] * (len(parts) + 4),
         out_specs=[vmem] * 2,
         compiler_params=pltpu.CompilerParams(vmem_limit_bytes=8 * MIB),
         cost_estimate=pl.CostEstimate(flops=67_000_000, bytes_accessed=MIB, transcendentals=0),
         name="query",
-    )(*parts, query_weight)
+    )(*parts, query_weight, key_weight, value_weight, out_weight)
     operands = [
         sink_logit,
         norm_gain.reshape(1, width),

time: 56.3 us -> 55.6 us (0.988)
  local copies, waits for them, and re-layouts: 1.38 us -> 0.7 us
    unnamed x11, local copies, waits for them, and re-layouts: 1.36 us -> 0.68 us
where the time goes in v5:
time: 55.6 us; the launch traced here: 55.3 us
  starting transfers between devices  26.5 us (48%)
  blocking collectives  13.1 us (24%)
  waiting for transfers between devices  8.37 us (15%)
  Pallas kernels  6.35 us (11%)
  local copies, waits for them, and re-layouts  0.7 us (1%)
    ppermute x4, starting transfers between devices, exchange_permute(): return lax.ppermute(array, 'lev', [(i, i ^ offset) for i in range(count)])  14 us
    all_to_all x1, blocking collectives, body(): lax.all_to_all(encoded.reshape(levels, cells_here, width), 'lev', split_a...  13.1 us
    all_to_all x1, starting transfers between devices, body(): lax.all_to_all(bank.reshape(tile_count, capacity, token_width), 'tile', s...  12.5 us
    ppermute x4, waiting for transfers between devices, exchange_permute(): return lax.ppermute(array, 'lev', [(i, i ^ offset) for i in range(count)])  8.36 us
    pallas_call x1, Pallas kernels, body(): pl.pallas_call(functools.partial(encode_kernel, block_order=[o ^ first fo...  3.64 us
    pallas_call x1, Pallas kernels, body(): route([bank_shape, half_shape])(*of)  1.43 us
  transfers between devices with their start and end apart: 5, of which 3 were waited for; matrix products, arithmetic and copies ran while one was open for 0% of the time, Pallas kernels for 0%

profile of v5, /device:TPU:198, one launch (start us, length us, event | category | flops | bytes accessed | tf_op | source)
XLA Modules:
  0.0 55.3 jit_solution(3388711110467215326)
XLA Ops:
  0.0 1.0 %fetch.1 = (bf16[4,16,512]{2,1,0:T(8,128)(2,1)S(1)}, s32[1,512]{1,0:T(1,128)S(1)}, s32[1,512]{1,0:T(1,128)S(1)}, bf16[512,256]{1,0:T(8,128)(2,1)S(1)}) custom-call(s32[1]{0:T(128)} %bitcast.level_here.refs_0_, bf16[8,16,512]{2,1,0:T(8,128)(2,1)} %bitcast.18, s32[1,512]{1,0:T(1,128)} %bitcast.23, s32[1,512]{1,0:T(1,128)} %bitcast.24, bf16[512,256]{1,0:T(8,128)(2,1)} %tokens_hbm.1), custom_call_target="tpu_custom_call" | custom-call | flops 1000 | bytes 1048576 | tf_op jit(solution)/shard_map/fetch/pallas_call | solution.py:220
  1.1 1.4 %conditional.2 = ((bf16[1024,256]{1,0:T(8,128)(2,1)}, bf16[4,16,512]{2,1,0:T(8,128)(2,1)})) conditional(s32[]{:T(128)} %convert_element_type.4, (s32[1]{0:T(128)}, s32[1,512]{1,0:T(1,128)S(1)}, s32[1,512]{1,0:T(1,128)S(1)}, bf16[512,256]{1,0:T(8,128)(2,1)S(1)}) %tuple.18, (s32[1]{0:T(128)}, s32[1,512]{1,0:T(1,128)S(1)}, s32[1,512]{1,0:T(1,128)S(1)}, ...), branch_computations={%region_0.1_spmd, %region_1.2_spmd} | conditional | flops 300000000 | bytes 1310784 | solution.py:263
  1.1 1.4 %route.2 = (bf16[1024,256]{1,0:T(8,128)(2,1)}, bf16[4,16,512]{2,1,0:T(8,128)(2,1)}) custom-call(s32[1]{0:T(128)} %get-tuple-element.27.sub_here, s32[1,512]{1,0:T(1,128)S(1)} %get-tuple-element.28.target_ref, s32[1,512]{1,0:T(1,128)S(1)} %get-tuple-element.29.subtile_ref, bf16[512,256]{1,0:T(8,128)(2,1)S(1)} %get-tuple-element.30.tokens_ref), custom_call_target="tpu_custom_call" | custom-call | flops 300000000 | bytes 1048576 | tf_op jit(solution)/shard_map/cond/branch_0_fun/route/pallas_call | solution.py:266
  2.5 0.0 copy-start.4
  2.5 0.0 copy-start.1
  2.5 0.0 copy-start.3
  2.5 12.5 %all-to-all-start = ((bf16[64,16,256]{2,1,0:T(8,128)(2,1)}), bf16[64,16,256]{2,1,0:T(8,128)(2,1)S(1)}, u32[]{:S(2)}, u32[]{:S(2)}) async-start(bf16[64,16,256]{2,1,0:T(8,128)(2,1)} %bitcast.5), calls=%async_computation | async-start | bytes 1048576 | tf_op jit(solution)/shard_map/all_to_all | solution.py:274
  15.1 0.0 copy-start
  15.1 6.3 %conditional.3 = (bf16[4,16,512]{2,1,0:T(8,128)(2,1)S(1)}) conditional(s32[]{:T(128)} %convert_element_type.4, bf16[4,16,512]{2,1,0:T(8,128)(2,1)S(1)} %get-tuple-element.47, () %tuple.20), branch_computations={%region_2.3_spmd, %region_3.4_spmd} | conditional | bytes 262192 | solution.py:281
  15.1 2.6 %collective-permute-start.1 = (bf16[4,16,512]{2,1,0:T(8,128)(2,1)S(1)}, bf16[4,16,512]{2,1,0:T(8,128)(2,1)S(1)}, u32[]{:S(2)}, u32[]{:S(2)}) collective-permute-start(bf16[4,16,512]{2,1,0:T(8,128)(2,1)S(1)} %param.2), channel_id=1, source_target_pairs={{0,1},{1,0},{2,3},{3,2},{4,5},{5,4},{6,7},{7,6},{8,9},{9,8},{10,11... | collective-permute-start | bytes 196616 | tf_op jit(solution)/shard_map/cond/branch_0_fun/ppermute | solution.py:188
  17.7 3.7 %collective-permute-done.1 = bf16[4,16,512]{2,1,0:T(8,128)(2,1)S(1)} collective-permute-done((bf16[4,16,512]{2,1,0:T(8,128)(2,1)S(1)}, bf16[4,16,512]{2,1,0:T(8,128)(2,1)S(1)}, u32[]{:S(2)}, u32[]{:S(2)}) %collective-permute-start.1) | collective-permute-done | bytes 65568 | tf_op jit(solution)/shard_map/cond/branch_0_fun/ppermute | solution.py:188
  21.4 0.0 copy-done.4
  21.4 0.0 copy-start.2
  21.5 6.0 %collective-permute-start.4 = (bf16[32,512]{1,0:T(8,128)(2,1)S(1)}, bf16[32,512]{1,0:T(8,128)(2,1)S(1)}, u32[]{:S(2)}, u32[]{:S(2)}) collective-permute-start(bf16[32,512]{1,0:T(8,128)(2,1)S(1)} %bitcast.20), channel_id=1, source_target_pairs={{0,5},{1,4},{2,7},{3,6},{4,1},{5,0},{6,3},{7,2},{8,13},{9,12},{10,... | collective-permute-start | bytes 98312 | tf_op jit(solution)/shard_map/ppermute | solution.py:188
  27.5 3.1 %collective-permute-start.3 = (bf16[32,512]{1,0:T(8,128)(2,1)S(1)}, bf16[32,512]{1,0:T(8,128)(2,1)S(1)}, u32[]{:S(2)}, u32[]{:S(2)}) collective-permute-start(bf16[32,512]{1,0:T(8,128)(2,1)S(1)} %bitcast.21), channel_id=1, source_target_pairs={{0,6},{1,7},{2,4},{3,5},{4,2},{5,3},{6,0},{7,1},{8,14},{9,15},{10,... | collective-permute-start | bytes 98312 | tf_op jit(solution)/shard_map/ppermute | solution.py:188
  30.7 2.3 %collective-permute-start.2 = (bf16[32,512]{1,0:T(8,128)(2,1)S(1)}, bf16[32,512]{1,0:T(8,128)(2,1)S(1)}, u32[]{:S(2)}, u32[]{:S(2)}) collective-permute-start(bf16[32,512]{1,0:T(8,128)(2,1)S(1)} %bitcast.22), channel_id=1, source_target_pairs={{0,2},{1,3},{2,0},{3,1},{4,6},{5,7},{6,4},{7,5},{8,10},{9,11},{10,... | collective-permute-start | bytes 98312 | tf_op jit(solution)/shard_map/ppermute | solution.py:188
  33.0 0.0 collective-permute-done.4.refs_3_
  33.0 2.6 %collective-permute-done.3.refs_2_ = bf16[32,512]{1,0:T(8,128)(2,1)S(1)} collective-permute-done((bf16[32,512]{1,0:T(8,128)(2,1)S(1)}, bf16[32,512]{1,0:T(8,128)(2,1)S(1)}, u32[]{:S(2)}, u32[]{:S(2)}) %collective-permute-start.3) | collective-permute-done | bytes 32800 | tf_op jit(solution)/shard_map/ppermute | solution.py:188
  35.5 2.1 %collective-permute-done.2.refs_1_ = bf16[32,512]{1,0:T(8,128)(2,1)S(1)} collective-permute-done((bf16[32,512]{1,0:T(8,128)(2,1)S(1)}, bf16[32,512]{1,0:T(8,128)(2,1)S(1)}, u32[]{:S(2)}, u32[]{:S(2)}) %collective-permute-start.2) | collective-permute-done | bytes 32800 | tf_op jit(solution)/shard_map/ppermute | solution.py:188
  37.6 0.0 copy-done.1
  37.6 0.0 copy-done.3
  37.6 0.0 copy-done
  37.6 0.0 copy-done.2
  37.6 0.2 query.1
  37.9 0.0 all-to-all-done
  37.9 3.6 %encode.1 = bf16[128,512]{1,0:T(8,128)(2,1)S(1)} custom-call(s32[1]{0:T(128)} %bitcast.level_here.refs_0_, bf16[1024,256]{1,0:T(8,128)(2,1)S(1)} %bitcast.14, bf16[256,512]{1,0:T(8,128)(2,1)S(1)} %copy-done.2, bf16[256,512]{1,0:T(8,128)(2,1)S(1)} %copy-done.3, bf16[512,512]{1,0:T(8,128)(2,1)S(1)} %copy-done.1, ...), custom_call_target="tpu_custom_call" | custom-call | flops 1500000000 | bytes 5242880 | tf_op jit(solution)/shard_map/encode/pallas_call | solution.py:307
  41.5 13.1 %all_to_all.17 = bf16[8,16,512]{2,1,0:T(8,128)(2,1)S(1)} all-to-all(bf16[8,16,512]{2,1,0:T(8,128)(2,1)S(1)} %bitcast.15), channel_id=1, replica_groups=mesh['tile'=64,'lev'=8] {'lev'}, dimensions={0} | all-to-all | bytes 262144 | tf_op jit(solution)/shard_map/all_to_all | solution.py:325
  54.6 0.7 %copy.21 = bf16[1,128,512]{2,1,0:T(8,128)(2,1)} copy(bf16[1,128,512]{2,1,0:T(8,128)(2,1)S(1)} %bitcast.17) | data formatting | bytes 262144
  (6 shorter events, 0.1 us)
Async XLA Ops:
  2.5 18.9 %copy-start.4 = (bf16[1,128,512]{2,1,0:T(8,128)(2,1)S(1)}, bf16[1,128,512]{2,1,0:T(8,128)(2,1)}, u32[]{:S(2)}) copy-start(bf16[1,128,512]{2,1,0:T(8,128)(2,1)} %param.17) | copy-start | bytes 393220
  2.5 35.1 %copy-start.1 = (bf16[512,512]{1,0:T(8,128)(2,1)S(1)}, bf16[512,512]{1,0:T(8,128)(2,1)}, u32[]{:S(2)}) copy-start(bf16[512,512]{1,0:T(8,128)(2,1)} %refs_4_.3) | copy-start | bytes 1572868
  2.5 35.1 %copy-start.3 = (bf16[256,512]{1,0:T(8,128)(2,1)S(1)}, bf16[256,512]{1,0:T(8,128)(2,1)}, u32[]{:S(2)}) copy-start(bf16[256,512]{1,0:T(8,128)(2,1)} %refs_3_.1) | copy-start | bytes 786436
  2.5 35.4 %all-to-all-start = ((bf16[64,16,256]{2,1,0:T(8,128)(2,1)}), bf16[64,16,256]{2,1,0:T(8,128)(2,1)S(1)}, u32[]{:S(2)}, u32[]{:S(2)}) async-start(bf16[64,16,256]{2,1,0:T(8,128)(2,1)} %bitcast.5), calls=%async_computation | async-start | bytes 1048576 | tf_op jit(solution)/shard_map/all_to_all | solution.py:274
  15.1 22.6 %copy-start = (bf16[512,512]{1,0:T(8,128)(2,1)S(1)}, bf16[512,512]{1,0:T(8,128)(2,1)}, u32[]{:S(2)}) copy-start(bf16[512,512]{1,0:T(8,128)(2,1)} %refs_4_.2) | copy-start | bytes 1572868
  15.1 6.3 %collective-permute-start.1 = (bf16[4,16,512]{2,1,0:T(8,128)(2,1)S(1)}, bf16[4,16,512]{2,1,0:T(8,128)(2,1)S(1)}, u32[]{:S(2)}, u32[]{:S(2)}) collective-permute-start(bf16[4,16,512]{2,1,0:T(8,128)(2,1)S(1)} %param.2), channel_id=1, source_target_pairs={{0,1},{1,0},{2,3},{3,2},{4,5},{5,4},{6,7},{7,6},{8,9},{9,8},{10,11... | collective-permute-start | bytes 196616 | tf_op jit(solution)/shard_map/cond/branch_0_fun/ppermute | solution.py:188
  21.4 16.2 %copy-start.2 = (bf16[256,512]{1,0:T(8,128)(2,1)S(1)}, bf16[256,512]{1,0:T(8,128)(2,1)}, u32[]{:S(2)}) copy-start(bf16[256,512]{1,0:T(8,128)(2,1)} %refs_2_.1) | copy-start | bytes 786436
  21.5 11.5 %collective-permute-start.4 = (bf16[32,512]{1,0:T(8,128)(2,1)S(1)}, bf16[32,512]{1,0:T(8,128)(2,1)S(1)}, u32[]{:S(2)}, u32[]{:S(2)}) collective-permute-start(bf16[32,512]{1,0:T(8,128)(2,1)S(1)} %bitcast.20), channel_id=1, source_target_pairs={{0,5},{1,4},{2,7},{3,6},{4,1},{5,0},{6,3},{7,2},{8,13},{9,12},{10,... | collective-permute-start | bytes 98312 | tf_op jit(solution)/shard_map/ppermute | solution.py:188
  27.5 8.0 %collective-permute-start.3 = (bf16[32,512]{1,0:T(8,128)(2,1)S(1)}, bf16[32,512]{1,0:T(8,128)(2,1)S(1)}, u32[]{:S(2)}, u32[]{:S(2)}) collective-permute-start(bf16[32,512]{1,0:T(8,128)(2,1)S(1)} %bitcast.21), channel_id=1, source_target_pairs={{0,6},{1,7},{2,4},{3,5},{4,2},{5,3},{6,0},{7,1},{8,14},{9,15},{10,... | collective-permute-start | bytes 98312 | tf_op jit(solution)/shard_map/ppermute | solution.py:188
  30.7 6.9 %collective-permute-start.2 = (bf16[32,512]{1,0:T(8,128)(2,1)S(1)}, bf16[32,512]{1,0:T(8,128)(2,1)S(1)}, u32[]{:S(2)}, u32[]{:S(2)}) collective-permute-start(bf16[32,512]{1,0:T(8,128)(2,1)S(1)} %bitcast.22), channel_id=1, source_target_pairs={{0,2},{1,3},{2,0},{3,1},{4,6},{5,7},{6,4},{7,5},{8,10},{9,11},{10,... | collective-permute-start | bytes 98312 | tf_op jit(solution)/shard_map/ppermute | solution.py:188

commit v6 on v5

--- a/solution.py
+++ b/solution.py
@@ -15,7 +15,7 @@
 
 
 FIRST = 1
-LATER = (0, 2, 6, 5)
+LATER = (0, 2, 5, 6)
 
 
 def pick(pieces, levels):

time: 55.6 us -> 55.7 us (level)
  no operation moved by 1% of the time
where the time goes in v6:
time: 55.7 us; the launch traced here: 55.3 us
  starting transfers between devices  26.5 us (48%)
  blocking collectives  13.1 us (24%)
  waiting for transfers between devices  8.37 us (15%)
  Pallas kernels  6.35 us (11%)
  local copies, waits for them, and re-layouts  0.7 us (1%)
    ppermute x4, starting transfers between devices, exchange_permute(): return lax.ppermute(array, 'lev', [(i, i ^ offset) for i in range(count)])  14 us
    all_to_all x1, blocking collectives, body(): lax.all_to_all(encoded.reshape(levels, cells_here, width), 'lev', split_a...  13.1 us
    all_to_all x1, starting transfers between devices, body(): lax.all_to_all(bank.reshape(tile_count, capacity, token_width), 'tile', s...  12.5 us
    ppermute x4, waiting for transfers between devices, exchange_permute(): return lax.ppermute(array, 'lev', [(i, i ^ offset) for i in range(count)])  8.36 us
    pallas_call x1, Pallas kernels, body(): pl.pallas_call(functools.partial(encode_kernel, block_order=[o ^ first fo...  3.64 us
    pallas_call x1, Pallas kernels, body(): route([bank_shape, half_shape])(*of)  1.43 us
  transfers between devices with their start and end apart: 5, of which 3 were waited for; matrix products, arithmetic and copies ran while one was open for 0% of the time, Pallas kernels for 0%

profile of v6, /device:TPU:198, one launch (start us, length us, event | category | flops | bytes accessed | tf_op | source)
XLA Modules:
  0.0 55.3 jit_solution(8283751442039878037)
XLA Ops:
  0.0 1.0 %fetch.1 = (bf16[4,16,512]{2,1,0:T(8,128)(2,1)S(1)}, s32[1,512]{1,0:T(1,128)S(1)}, s32[1,512]{1,0:T(1,128)S(1)}, bf16[512,256]{1,0:T(8,128)(2,1)S(1)}) custom-call(s32[1]{0:T(128)} %bitcast.level_here.refs_0_, bf16[8,16,512]{2,1,0:T(8,128)(2,1)} %bitcast.18, s32[1,512]{1,0:T(1,128)} %bitcast.23, s32[1,512]{1,0:T(1,128)} %bitcast.24, bf16[512,256]{1,0:T(8,128)(2,1)} %tokens_hbm.1), custom_call_target="tpu_custom_call" | custom-call | flops 1000 | bytes 1048576 | tf_op jit(solution)/shard_map/fetch/pallas_call | solution.py:220
  1.1 1.4 %conditional.2 = ((bf16[1024,256]{1,0:T(8,128)(2,1)}, bf16[4,16,512]{2,1,0:T(8,128)(2,1)})) conditional(s32[]{:T(128)} %convert_element_type.4, (s32[1]{0:T(128)}, s32[1,512]{1,0:T(1,128)S(1)}, s32[1,512]{1,0:T(1,128)S(1)}, bf16[512,256]{1,0:T(8,128)(2,1)S(1)}) %tuple.18, (s32[1]{0:T(128)}, s32[1,512]{1,0:T(1,128)S(1)}, s32[1,512]{1,0:T(1,128)S(1)}, ...), branch_computations={%region_0.1_spmd, %region_1.2_spmd} | conditional | flops 300000000 | bytes 1310784 | solution.py:263
  1.1 1.4 %route.2 = (bf16[1024,256]{1,0:T(8,128)(2,1)}, bf16[4,16,512]{2,1,0:T(8,128)(2,1)}) custom-call(s32[1]{0:T(128)} %get-tuple-element.27.sub_here, s32[1,512]{1,0:T(1,128)S(1)} %get-tuple-element.28.target_ref, s32[1,512]{1,0:T(1,128)S(1)} %get-tuple-element.29.subtile_ref, bf16[512,256]{1,0:T(8,128)(2,1)S(1)} %get-tuple-element.30.tokens_ref), custom_call_target="tpu_custom_call" | custom-call | flops 300000000 | bytes 1048576 | tf_op jit(solution)/shard_map/cond/branch_0_fun/route/pallas_call | solution.py:266
  2.5 0.0 copy-start.4
  2.5 0.0 copy-start.1
  2.5 0.0 copy-start.3
  2.5 12.5 %all-to-all-start = ((bf16[64,16,256]{2,1,0:T(8,128)(2,1)}), bf16[64,16,256]{2,1,0:T(8,128)(2,1)S(1)}, u32[]{:S(2)}, u32[]{:S(2)}) async-start(bf16[64,16,256]{2,1,0:T(8,128)(2,1)} %bitcast.5), calls=%async_computation | async-start | bytes 1048576 | tf_op jit(solution)/shard_map/all_to_all | solution.py:274
  15.1 0.0 copy-start
  15.1 6.3 %conditional.3 = (bf16[4,16,512]{2,1,0:T(8,128)(2,1)S(1)}) conditional(s32[]{:T(128)} %convert_element_type.4, bf16[4,16,512]{2,1,0:T(8,128)(2,1)S(1)} %get-tuple-element.47, () %tuple.20), branch_computations={%region_2.3_spmd, %region_3.4_spmd} | conditional | bytes 262192 | solution.py:281
  15.1 2.6 %collective-permute-start.1 = (bf16[4,16,512]{2,1,0:T(8,128)(2,1)S(1)}, bf16[4,16,512]{2,1,0:T(8,128)(2,1)S(1)}, u32[]{:S(2)}, u32[]{:S(2)}) collective-permute-start(bf16[4,16,512]{2,1,0:T(8,128)(2,1)S(1)} %param.2), channel_id=1, source_target_pairs={{0,1},{1,0},{2,3},{3,2},{4,5},{5,4},{6,7},{7,6},{8,9},{9,8},{10,11... | collective-permute-start | bytes 196616 | tf_op jit(solution)/shard_map/cond/branch_0_fun/ppermute | solution.py:188
  17.7 3.7 %collective-permute-done.1 = bf16[4,16,512]{2,1,0:T(8,128)(2,1)S(1)} collective-permute-done((bf16[4,16,512]{2,1,0:T(8,128)(2,1)S(1)}, bf16[4,16,512]{2,1,0:T(8,128)(2,1)S(1)}, u32[]{:S(2)}, u32[]{:S(2)}) %collective-permute-start.1) | collective-permute-done | bytes 65568 | tf_op jit(solution)/shard_map/cond/branch_0_fun/ppermute | solution.py:188
  21.4 0.0 copy-done.4
  21.4 0.0 copy-start.2
  21.5 5.3 %collective-permute-start.4 = (bf16[32,512]{1,0:T(8,128)(2,1)S(1)}, bf16[32,512]{1,0:T(8,128)(2,1)S(1)}, u32[]{:S(2)}, u32[]{:S(2)}) collective-permute-start(bf16[32,512]{1,0:T(8,128)(2,1)S(1)} %bitcast.20), channel_id=1, source_target_pairs={{0,6},{1,7},{2,4},{3,5},{4,2},{5,3},{6,0},{7,1},{8,14},{9,15},{10,... | collective-permute-start | bytes 98312 | tf_op jit(solution)/shard_map/ppermute | solution.py:188
  26.7 3.9 %collective-permute-start.3 = (bf16[32,512]{1,0:T(8,128)(2,1)S(1)}, bf16[32,512]{1,0:T(8,128)(2,1)S(1)}, u32[]{:S(2)}, u32[]{:S(2)}) collective-permute-start(bf16[32,512]{1,0:T(8,128)(2,1)S(1)} %bitcast.21), channel_id=1, source_target_pairs={{0,5},{1,4},{2,7},{3,6},{4,1},{5,0},{6,3},{7,2},{8,13},{9,12},{10,... | collective-permute-start | bytes 98312 | tf_op jit(solution)/shard_map/ppermute | solution.py:188
  30.7 2.3 %collective-permute-start.2 = (bf16[32,512]{1,0:T(8,128)(2,1)S(1)}, bf16[32,512]{1,0:T(8,128)(2,1)S(1)}, u32[]{:S(2)}, u32[]{:S(2)}) collective-permute-start(bf16[32,512]{1,0:T(8,128)(2,1)S(1)} %bitcast.22), channel_id=1, source_target_pairs={{0,2},{1,3},{2,0},{3,1},{4,6},{5,7},{6,4},{7,5},{8,10},{9,11},{10,... | collective-permute-start | bytes 98312 | tf_op jit(solution)/shard_map/ppermute | solution.py:188
  33.0 0.0 collective-permute-done.4.refs_3_
  33.0 2.7 %collective-permute-done.3.refs_2_ = bf16[32,512]{1,0:T(8,128)(2,1)S(1)} collective-permute-done((bf16[32,512]{1,0:T(8,128)(2,1)S(1)}, bf16[32,512]{1,0:T(8,128)(2,1)S(1)}, u32[]{:S(2)}, u32[]{:S(2)}) %collective-permute-start.3) | collective-permute-done | bytes 32800 | tf_op jit(solution)/shard_map/ppermute | solution.py:188
  35.7 2.0 %collective-permute-done.2.refs_1_ = bf16[32,512]{1,0:T(8,128)(2,1)S(1)} collective-permute-done((bf16[32,512]{1,0:T(8,128)(2,1)S(1)}, bf16[32,512]{1,0:T(8,128)(2,1)S(1)}, u32[]{:S(2)}, u32[]{:S(2)}) %collective-permute-start.2) | collective-permute-done | bytes 32800 | tf_op jit(solution)/shard_map/ppermute | solution.py:188
  37.6 0.0 copy-done.1
  37.6 0.0 copy-done.3
  37.6 0.0 copy-done
  37.6 0.0 copy-done.2
  37.6 0.2 query.1
  37.9 0.0 all-to-all-done
  37.9 3.6 %encode.1 = bf16[128,512]{1,0:T(8,128)(2,1)S(1)} custom-call(s32[1]{0:T(128)} %bitcast.level_here.refs_0_, bf16[1024,256]{1,0:T(8,128)(2,1)S(1)} %bitcast.14, bf16[256,512]{1,0:T(8,128)(2,1)S(1)} %copy-done.2, bf16[256,512]{1,0:T(8,128)(2,1)S(1)} %copy-done.3, bf16[512,512]{1,0:T(8,128)(2,1)S(1)} %copy-done.1, ...), custom_call_target="tpu_custom_call" | custom-call | flops 1500000000 | bytes 5242880 | tf_op jit(solution)/shard_map/encode/pallas_call | solution.py:307
  41.5 13.1 %all_to_all.17 = bf16[8,16,512]{2,1,0:T(8,128)(2,1)S(1)} all-to-all(bf16[8,16,512]{2,1,0:T(8,128)(2,1)S(1)} %bitcast.15), channel_id=1, replica_groups=mesh['tile'=64,'lev'=8] {'lev'}, dimensions={0} | all-to-all | bytes 262144 | tf_op jit(solution)/shard_map/all_to_all | solution.py:325
  54.6 0.7 %copy.21 = bf16[1,128,512]{2,1,0:T(8,128)(2,1)} copy(bf16[1,128,512]{2,1,0:T(8,128)(2,1)S(1)} %bitcast.17) | data formatting | bytes 262144
  (6 shorter events, 0.1 us)
Async XLA Ops:
  2.5 18.9 %copy-start.4 = (bf16[1,128,512]{2,1,0:T(8,128)(2,1)S(1)}, bf16[1,128,512]{2,1,0:T(8,128)(2,1)}, u32[]{:S(2)}) copy-start(bf16[1,128,512]{2,1,0:T(8,128)(2,1)} %param.17) | copy-start | bytes 393220
  2.5 35.1 %copy-start.1 = (bf16[512,512]{1,0:T(8,128)(2,1)S(1)}, bf16[512,512]{1,0:T(8,128)(2,1)}, u32[]{:S(2)}) copy-start(bf16[512,512]{1,0:T(8,128)(2,1)} %refs_4_.3) | copy-start | bytes 1572868
  2.5 35.1 %copy-start.3 = (bf16[256,512]{1,0:T(8,128)(2,1)S(1)}, bf16[256,512]{1,0:T(8,128)(2,1)}, u32[]{:S(2)}) copy-start(bf16[256,512]{1,0:T(8,128)(2,1)} %refs_3_.1) | copy-start | bytes 786436
  2.5 35.4 %all-to-all-start = ((bf16[64,16,256]{2,1,0:T(8,128)(2,1)}), bf16[64,16,256]{2,1,0:T(8,128)(2,1)S(1)}, u32[]{:S(2)}, u32[]{:S(2)}) async-start(bf16[64,16,256]{2,1,0:T(8,128)(2,1)} %bitcast.5), calls=%async_computation | async-start | bytes 1048576 | tf_op jit(solution)/shard_map/all_to_all | solution.py:274
  15.1 22.6 %copy-start = (bf16[512,512]{1,0:T(8,128)(2,1)S(1)}, bf16[512,512]{1,0:T(8,128)(2,1)}, u32[]{:S(2)}) copy-start(bf16[512,512]{1,0:T(8,128)(2,1)} %refs_4_.2) | copy-start | bytes 1572868
  15.1 6.3 %collective-permute-start.1 = (bf16[4,16,512]{2,1,0:T(8,128)(2,1)S(1)}, bf16[4,16,512]{2,1,0:T(8,128)(2,1)S(1)}, u32[]{:S(2)}, u32[]{:S(2)}) collective-permute-start(bf16[4,16,512]{2,1,0:T(8,128)(2,1)S(1)} %param.2), channel_id=1, source_target_pairs={{0,1},{1,0},{2,3},{3,2},{4,5},{5,4},{6,7},{7,6},{8,9},{9,8},{10,11... | collective-permute-start | bytes 196616 | tf_op jit(solution)/shard_map/cond/branch_0_fun/ppermute | solution.py:188
  21.4 16.2 %copy-start.2 = (bf16[256,512]{1,0:T(8,128)(2,1)S(1)}, bf16[256,512]{1,0:T(8,128)(2,1)}, u32[]{:S(2)}) copy-start(bf16[256,512]{1,0:T(8,128)(2,1)} %refs_2_.1) | copy-start | bytes 786436
  21.5 11.5 %collective-permute-start.4 = (bf16[32,512]{1,0:T(8,128)(2,1)S(1)}, bf16[32,512]{1,0:T(8,128)(2,1)S(1)}, u32[]{:S(2)}, u32[]{:S(2)}) collective-permute-start(bf16[32,512]{1,0:T(8,128)(2,1)S(1)} %bitcast.20), channel_id=1, source_target_pairs={{0,6},{1,7},{2,4},{3,5},{4,2},{5,3},{6,0},{7,1},{8,14},{9,15},{10,... | collective-permute-start | bytes 98312 | tf_op jit(solution)/shard_map/ppermute | solution.py:188
  26.7 8.9 %collective-permute-start.3 = (bf16[32,512]{1,0:T(8,128)(2,1)S(1)}, bf16[32,512]{1,0:T(8,128)(2,1)S(1)}, u32[]{:S(2)}, u32[]{:S(2)}) collective-permute-start(bf16[32,512]{1,0:T(8,128)(2,1)S(1)} %bitcast.21), channel_id=1, source_target_pairs={{0,5},{1,4},{2,7},{3,6},{4,1},{5,0},{6,3},{7,2},{8,13},{9,12},{10,... | collective-permute-start | bytes 98312 | tf_op jit(solution)/shard_map/ppermute | solution.py:188
  30.7 6.9 %collective-permute-start.2 = (bf16[32,512]{1,0:T(8,128)(2,1)S(1)}, bf16[32,512]{1,0:T(8,128)(2,1)S(1)}, u32[]{:S(2)}, u32[]{:S(2)}) collective-permute-start(bf16[32,512]{1,0:T(8,128)(2,1)S(1)} %bitcast.22), channel_id=1, source_target_pairs={{0,2},{1,3},{2,0},{3,1},{4,6},{5,7},{6,4},{7,5},{8,10},{9,11},{10,... | collective-permute-start | bytes 98312 | tf_op jit(solution)/shard_map/ppermute | solution.py:188

commit v7 on v3

--- a/solution.py
+++ b/solution.py
@@ -12,10 +12,11 @@
 EMPTY = 64.0
 EMPTY_FROM = 48.0
 MIB = 1 << 20
+GROUP = 8
 
 
 FIRST = 1
-LATER = (0, 5, 6, 2)
+LATER = (0, 6, 5, 2)
 
 
 def pick(pieces, levels):
@@ -29,16 +30,22 @@
     return loads
 
 
+def half_kernel(level_here, pieces_hbm, half_ref, loaded):
+    far = [pieces_hbm.at[level_here[0] ^ FIRST ^ offset] for offset in LATER]
+    for load in start_loads(far, [half_ref.at[i] for i in range(len(LATER))], loaded):
+        load.wait()
+
+
 def fetch_kernel(
     level_here,
-    pieces_hbm,
     target_hbm,
     subtile_hbm,
     tokens_hbm,
-    half_ref,
+    pieces_hbm,
     target_ref,
     subtile_ref,
     tokens_ref,
+    half_ref,
     loaded,
 ):
     far = [target_hbm, subtile_hbm, tokens_hbm]
@@ -50,22 +57,15 @@
         load.wait()
 
 
-def route_kernel(
-    sub_here,
-    target_ref,
-    subtile_ref,
-    tokens_ref,
-    bank_ref,
-    *,
-    tile_count,
-    capacity,
-):
+def fill_bank(sub_here, target_ref, subtile_ref, tokens_ref, bank_ref, loads, tile_count, capacity):
     rows = tokens_ref.shape[0]
     width = tokens_ref.shape[1]
     before = lax.broadcasted_iota(jnp.int32, (rows, rows), 0) < lax.broadcasted_iota(
         jnp.int32, (rows, rows), 1
     )
     before = jnp.where(before, 1.0, 0.0).astype(jnp.bfloat16)
+    for load in loads[:2]:
+        load.wait()
     keep = jnp.abs(subtile_ref[...] - sub_here[0]) <= 1
     target = jnp.where(keep, target_ref[...], -1)
     tile_ids = lax.broadcasted_iota(jnp.int32, (tile_count, rows), 0)
@@ -74,8 +74,10 @@
     rank = jnp.dot(onehot.astype(jnp.bfloat16), before, preferred_element_type=jnp.float32)
     rank = jnp.where(named, rank, -1.0)
     count = jnp.sum(onehot, axis=1, keepdims=True)
+    for load in loads[2:]:
+        load.wait()
     tokens = tokens_ref[...]
-    group = 8
+    group = GROUP
     slot = lax.broadcasted_iota(jnp.int32, (group, capacity, rows), 1).astype(jnp.float32)
     slot_out = lax.broadcasted_iota(jnp.int32, (group, capacity, width), 1).astype(jnp.float32)
     for first in range(0, tile_count, group):
@@ -89,8 +91,32 @@
         ).astype(jnp.bfloat16)
 
 
+def route_early_kernel(
+    sub_here,
+    target_hbm,
+    subtile_hbm,
+    tokens_hbm,
+    bank_ref,
+    target_ref,
+    subtile_ref,
+    tokens_ref,
+    loaded,
+    **sizes,
+):
+    near = (target_ref, subtile_ref, tokens_ref)
+    loads = start_loads((target_hbm, subtile_hbm, tokens_hbm), near, loaded)
+    fill_bank(sub_here, *near, bank_ref, loads, **sizes)
+
+
+def route_late_kernel(
+    sub_here, target_ref, subtile_ref, tokens_ref, half_ref, bank_ref, half_out_ref, **sizes
+):
+    half_out_ref[...] = half_ref[...]
+    fill_bank(sub_here, target_ref, subtile_ref, tokens_ref, bank_ref, [], **sizes)
+
+
 def query_kernel(*refs):
-    *piece_refs, weight_ref, columns_ref, query_ref = refs
+    *piece_refs, weight_ref, _, _, _, columns_ref, query_ref = refs
     columns = jnp.concatenate([ref[...] for ref in piece_refs], axis=0)
     columns_ref[...] = columns
     query = jnp.dot(columns, weight_ref[...], preferred_element_type=jnp.float32)
@@ -215,42 +241,81 @@
 
     here = lax.axis_index("lev")
     pieces = grid_state.reshape(levels, cells_here, width)
-    half, target, subtile_row, tokens = pl.pallas_call(
-        fetch_kernel,
-        out_shape=[
-            pltpu.VMEM((len(LATER), cells_here, width), grid_state.dtype),
-            pltpu.VMEM((1, token_rows), jnp.int32),
-            pltpu.VMEM((1, token_rows), jnp.int32),
-            pltpu.VMEM(observations.shape, observations.dtype),
-        ],
-        in_specs=[smem] + [far] * 4,
-        out_specs=[vmem] * 4,
-        scratch_shapes=[pltpu.SemaphoreType.DMA((3 + len(LATER),))],
+    bank_shape = jax.ShapeDtypeStruct((tile_count * capacity, token_width), observations.dtype)
+    half_shape = jax.ShapeDtypeStruct((len(LATER), cells_here, width), grid_state.dtype)
+
+    sizes = dict(tile_count=tile_count, capacity=capacity)
+    near_shapes = [
+        pltpu.VMEM((1, token_rows), jnp.int32),
+        pltpu.VMEM((1, token_rows), jnp.int32),
+        pltpu.VMEM(observations.shape, observations.dtype),
+    ]
+    small = dict(
         compiler_params=pltpu.CompilerParams(vmem_limit_bytes=8 * MIB),
         cost_estimate=pl.CostEstimate(flops=1000, bytes_accessed=MIB, transcendentals=0),
-        name="fetch",
-    )(
-        here.reshape(1),
-        *(
-            pltpu.with_memory_space_constraint(o, pltpu.HBM)
-            for o in (
-                pieces,
-                destination.reshape(1, token_rows),
-                subtile.reshape(1, token_rows),
-                observations,
-            )
-        ),
-    )
-    came = exchange_permute(half, FIRST, levels)
-    bank = pl.pallas_call(
-        functools.partial(route_kernel, tile_count=tile_count, capacity=capacity),
-        out_shape=jax.ShapeDtypeStruct((tile_count * capacity, token_width), observations.dtype),
-        in_specs=[smem] + [vmem] * 3,
-        out_specs=vmem,
+    )
+    large = dict(
         compiler_params=pltpu.CompilerParams(vmem_limit_bytes=32 * MIB),
         cost_estimate=pl.CostEstimate(flops=300_000_000, bytes_accessed=MIB, transcendentals=0),
-        name="route",
-    )(sub_here, target, subtile_row, tokens)
+    )
+
+    def in_hbm(arrays):
+        return [pltpu.with_memory_space_constraint(a, pltpu.HBM) for a in arrays]
+
+    def route_early(level, sub, *arrays):
+        half = pl.pallas_call(
+            half_kernel,
+            out_shape=half_shape,
+            in_specs=[smem, far],
+            out_specs=vmem,
+            scratch_shapes=[pltpu.SemaphoreType.DMA((len(LATER),))],
+            name="half",
+            **small,
+        )(level, *in_hbm(arrays[3:]))
+        came = exchange_permute(half, FIRST, levels)
+        bank = pl.pallas_call(
+            functools.partial(route_early_kernel, **sizes),
+            out_shape=bank_shape,
+            in_specs=[smem] + [far] * 3,
+            out_specs=vmem,
+            scratch_shapes=near_shapes + [pltpu.SemaphoreType.DMA((3,))],
+            name="route_early",
+            **large,
+        )(sub, *in_hbm(arrays[:3]))
+        return bank, came
+
+    def route_late(level, sub, *arrays):
+        near = pl.pallas_call(
+            fetch_kernel,
+            out_shape=near_shapes + [pltpu.VMEM(half_shape.shape, half_shape.dtype)],
+            in_specs=[smem] + [far] * 4,
+            out_specs=[vmem] * 4,
+            scratch_shapes=[pltpu.SemaphoreType.DMA((3 + len(LATER),))],
+            name="fetch",
+            **small,
+        )(level, *in_hbm(arrays))
+        bank, half = pl.pallas_call(
+            functools.partial(route_late_kernel, **sizes),
+            out_shape=[bank_shape, half_shape],
+            in_specs=[smem] + [vmem] * 4,
+            out_specs=[vmem] * 2,
+            name="route_late",
+            **large,
+        )(sub, *near)
+        return bank, half
+
+    early = (lax.axis_index("tile") // 2) % 8 < 3
+    bank, came = lax.cond(
+        early,
+        route_early,
+        route_late,
+        here.reshape(1),
+        sub_here,
+        destination.reshape(1, token_rows),
+        subtile.reshape(1, token_rows),
+        observations,
+        pieces,
+    )
     bank, came = lax.optimization_barrier((bank, came))
     received = lax.all_to_all(
         bank.reshape(tile_count, capacity, token_width),
@@ -259,6 +324,10 @@
         concat_axis=0,
         tiled=True,
     ).reshape(tile_count * capacity, token_width)
+    came_late = lax.cond(
+        early, jnp.zeros_like, lambda h: exchange_permute(h, FIRST, levels), came
+    )
+    came = jnp.where(early, came, came_late)
     parts = []
     for came_block, offset in zip(came, LATER):
         both = jnp.stack([pick(pieces, [here ^ offset])[0], came_block])
@@ -267,12 +336,12 @@
     columns, queries = pl.pallas_call(
         query_kernel,
         out_shape=[jax.ShapeDtypeStruct((rows, width), jnp.bfloat16)] * 2,
-        in_specs=[vmem] * (len(parts) + 1),
+        in_specs=[vmem] * (len(parts) + 4),
         out_specs=[vmem] * 2,
         compiler_params=pltpu.CompilerParams(vmem_limit_bytes=8 * MIB),
         cost_estimate=pl.CostEstimate(flops=67_000_000, bytes_accessed=MIB, transcendentals=0),
         name="query",
-    )(*parts, query_weight)
+    )(*parts, query_weight, key_weight, value_weight, out_weight)
     operands = [
         sink_logit,
         norm_gain.reshape(1, width),

time: 59.5 us -> 56 us (0.941)
  the two profiles are of different devices: /device:TPU:6 before, /device:TPU:198 now
where the time goes in v7:
time: 56 us; the launch traced here: 55.5 us
  starting transfers between devices  26.8 us (48%)
  blocking collectives  13.1 us (23%)
  waiting for transfers between devices  8.35 us (15%)
  Pallas kernels  6.36 us (11%)
  local copies, waits for them, and re-layouts  0.7 us (1%)
    ppermute x4, starting transfers between devices, exchange_permute(): return lax.ppermute(array, 'lev', [(i, i ^ offset) for i in range(count)])  14.5 us
    all_to_all x1, blocking collectives, body(): lax.all_to_all(encoded.reshape(levels, cells_here, width), 'lev', split_a...  13.1 us
    all_to_all x1, starting transfers between devices, body(): lax.all_to_all(bank.reshape(tile_count, capacity, token_width), 'tile', s...  12.3 us
    ppermute x4, waiting for transfers between devices, exchange_permute(): return lax.ppermute(array, 'lev', [(i, i ^ offset) for i in range(count)])  8.35 us
    pallas_call x1, Pallas kernels, body(): pl.pallas_call(functools.partial(encode_kernel, block_order=[o ^ first fo...  3.64 us
    pallas_call x1, Pallas kernels, route_late(): pl.pallas_call(functools.partial(route_late_kernel, **sizes), out_shape=[...  1.43 us
  transfers between devices with their start and end apart: 5, of which 3 were waited for; matrix products, arithmetic and copies ran while one was open for 0% of the time, Pallas kernels for 0%

profile of v7, /device:TPU:198, one launch (start us, length us, event | category | flops | bytes accessed | tf_op | source)
XLA Modules:
  0.0 55.5 jit_solution(5892297230717406020)
XLA Ops:
  0.0 2.5 %conditional.2 = ((bf16[1024,256]{1,0:T(8,128)(2,1)}, bf16[4,16,512]{2,1,0:T(8,128)(2,1)})) conditional(s32[]{:T(128)} %convert_element_type.4, (s32[1]{0:T(128)}, s32[1,512]{1,0:T(1,128)}, s32[1,512]{1,0:T(1,128)}, bf16[512,256]{1,0:T(8,128)(2,1)}, bf16[8,16,512]{2,1,0:T(8,128)(2,1)}, /*index=5*/s32[1]{0:T(128)}) %tuple.41, (s32[1]{0:T(128)}, ...), branch_computations={%region_0.1_spmd, %region_1.2_spmd} | conditional | flops 300000992 | bytes 2359360 | solution.py:308
  0.0 1.0 %fetch.1 = (s32[1,512]{1,0:T(1,128)S(1)}, s32[1,512]{1,0:T(1,128)S(1)}, bf16[512,256]{1,0:T(8,128)(2,1)S(1)}, bf16[4,16,512]{2,1,0:T(8,128)(2,1)S(1)}) custom-call(s32[1]{0:T(128)} %get-tuple-element.34.level_here, s32[1,512]{1,0:T(1,128)} %get-tuple-element.35.target_hbm, s32[1,512]{1,0:T(1,128)} %get-tuple-element.36.subtile_hbm, ...), custom_call_target="tpu_custom_call" | custom-call | flops 1000 | bytes 1048576 | tf_op jit(solution)/shard_map/cond/branch_0_fun/fetch/pallas_call | solution.py:288
  1.1 1.4 %route_late.1 = (bf16[1024,256]{1,0:T(8,128)(2,1)}, bf16[4,16,512]{2,1,0:T(8,128)(2,1)}) custom-call(s32[1]{0:T(128)} %get-tuple-element.33.sub_here, s32[1,512]{1,0:T(1,128)S(1)} %get-tuple-element.39.target_ref, s32[1,512]{1,0:T(1,128)S(1)} %get-tuple-element.40.subtile_ref, bf16[512,256]{1,0:T(8,128)(2,1)S(1)} %get-tuple-element.41.tokens_ref, ...), custom_call_target="tpu_custom_call" | custom-call | flops 300000000 | bytes 1048576 | tf_op jit(solution)/shard_map/cond/branch_0_fun/route_late/pallas_call | solution.py:297
  2.5 0.0 copy-start.4
  2.5 0.0 copy-start.1
  2.5 0.0 copy-start.3
  2.5 12.3 %all-to-all-start = ((bf16[64,16,256]{2,1,0:T(8,128)(2,1)}), bf16[64,16,256]{2,1,0:T(8,128)(2,1)S(1)}, u32[]{:S(2)}, u32[]{:S(2)}) async-start(bf16[64,16,256]{2,1,0:T(8,128)(2,1)} %bitcast.5), calls=%async_computation | async-start | bytes 1048576 | tf_op jit(solution)/shard_map/all_to_all | solution.py:320
  14.8 0.0 copy-start
  14.8 6.5 %conditional.3 = (bf16[4,16,512]{2,1,0:T(8,128)(2,1)S(1)}) conditional(s32[]{:T(128)} %convert_element_type.4, bf16[4,16,512]{2,1,0:T(8,128)(2,1)} %get-tuple-element.54, () %tuple.20), branch_computations={%region_2.3_spmd, %region_3.4_spmd} | conditional | bytes 262192 | solution.py:327
  14.8 2.8 %collective-permute-start.1 = (bf16[4,16,512]{2,1,0:T(8,128)(2,1)}, bf16[4,16,512]{2,1,0:T(8,128)(2,1)S(1)}, u32[]{:S(2)}, u32[]{:S(2)}) collective-permute-start(bf16[4,16,512]{2,1,0:T(8,128)(2,1)} %param.2), channel_id=1, source_target_pairs={{0,1},{1,0},{2,3},{3,2},{4,5},{5,4},{6,7},{7,6},{8,9},{9,8},{10,11... | collective-permute-start | bytes 196616 | tf_op jit(solution)/shard_map/cond/branch_0_fun/ppermute | solution.py:212
  17.6 3.7 %collective-permute-done.1 = bf16[4,16,512]{2,1,0:T(8,128)(2,1)S(1)} collective-permute-done((bf16[4,16,512]{2,1,0:T(8,128)(2,1)}, bf16[4,16,512]{2,1,0:T(8,128)(2,1)S(1)}, u32[]{:S(2)}, u32[]{:S(2)}) %collective-permute-start.1) | collective-permute-done | bytes 65568 | tf_op jit(solution)/shard_map/cond/branch_0_fun/ppermute | solution.py:212
  21.3 0.0 copy-done.4
  21.3 0.0 copy-start.2
  21.4 5.5 %collective-permute-start.2 = (bf16[32,512]{1,0:T(8,128)(2,1)S(1)}, bf16[32,512]{1,0:T(8,128)(2,1)S(1)}, u32[]{:S(2)}, u32[]{:S(2)}) collective-permute-start(bf16[32,512]{1,0:T(8,128)(2,1)S(1)} %bitcast.21), channel_id=1, source_target_pairs={{0,6},{1,7},{2,4},{3,5},{4,2},{5,3},{6,0},{7,1},{8,14},{9,15},{10,... | collective-permute-start | bytes 98312 | tf_op jit(solution)/shard_map/ppermute | solution.py:212
  26.9 3.9 %collective-permute-start.3 = (bf16[32,512]{1,0:T(8,128)(2,1)S(1)}, bf16[32,512]{1,0:T(8,128)(2,1)S(1)}, u32[]{:S(2)}, u32[]{:S(2)}) collective-permute-start(bf16[32,512]{1,0:T(8,128)(2,1)S(1)} %bitcast.22), channel_id=1, source_target_pairs={{0,5},{1,4},{2,7},{3,6},{4,1},{5,0},{6,3},{7,2},{8,13},{9,12},{10,... | collective-permute-start | bytes 98312 | tf_op jit(solution)/shard_map/ppermute | solution.py:212
  30.9 2.2 %collective-permute-start.4 = (bf16[32,512]{1,0:T(8,128)(2,1)S(1)}, bf16[32,512]{1,0:T(8,128)(2,1)S(1)}, u32[]{:S(2)}, u32[]{:S(2)}) collective-permute-start(bf16[32,512]{1,0:T(8,128)(2,1)S(1)} %bitcast.23), channel_id=1, source_target_pairs={{0,2},{1,3},{2,0},{3,1},{4,6},{5,7},{6,4},{7,5},{8,10},{9,11},{10,... | collective-permute-start | bytes 98312 | tf_op jit(solution)/shard_map/ppermute | solution.py:212
  33.1 0.0 collective-permute-done.2.refs_1_
  33.2 3.0 %collective-permute-done.3.refs_2_ = bf16[32,512]{1,0:T(8,128)(2,1)S(1)} collective-permute-done((bf16[32,512]{1,0:T(8,128)(2,1)S(1)}, bf16[32,512]{1,0:T(8,128)(2,1)S(1)}, u32[]{:S(2)}, u32[]{:S(2)}) %collective-permute-start.3) | collective-permute-done | bytes 32800 | tf_op jit(solution)/shard_map/ppermute | solution.py:212
  36.1 1.7 %collective-permute-done.4.refs_3_ = bf16[32,512]{1,0:T(8,128)(2,1)S(1)} collective-permute-done((bf16[32,512]{1,0:T(8,128)(2,1)S(1)}, bf16[32,512]{1,0:T(8,128)(2,1)S(1)}, u32[]{:S(2)}, u32[]{:S(2)}) %collective-permute-start.4) | collective-permute-done | bytes 32800 | tf_op jit(solution)/shard_map/ppermute | solution.py:212
  37.8 0.0 copy-done.1
  37.8 0.0 copy-done.3
  37.8 0.0 copy-done
  37.8 0.0 copy-done.2
  37.9 0.2 query.1
  38.1 0.0 all-to-all-done
  38.1 3.6 %encode.1 = bf16[128,512]{1,0:T(8,128)(2,1)S(1)} custom-call(s32[1]{0:T(128)} %bitcast.refs_0_, bf16[1024,256]{1,0:T(8,128)(2,1)S(1)} %bitcast.14, bf16[256,512]{1,0:T(8,128)(2,1)S(1)} %copy-done.2, bf16[256,512]{1,0:T(8,128)(2,1)S(1)} %copy-done.3, bf16[512,512]{1,0:T(8,128)(2,1)S(1)} %copy-done.1, bf16[128,512]{1,0:T(8,128)(2,1)S(1)} %get-tuple-element.55.refs_5_, ...), custom_call_target="tpu_custom_call" | custom-call | flops 1500000000 | bytes 5242880 | tf_op jit(solution)/shard_map/encode/pallas_call | solution.py:353
  41.8 13.1 %all_to_all.17 = bf16[8,16,512]{2,1,0:T(8,128)(2,1)S(1)} all-to-all(bf16[8,16,512]{2,1,0:T(8,128)(2,1)S(1)} %bitcast.15), channel_id=1, replica_groups=mesh['tile'=64,'lev'=8] {'lev'}, dimensions={0} | all-to-all | bytes 262144 | tf_op jit(solution)/shard_map/all_to_all | solution.py:371
  54.8 0.7 %copy.21 = bf16[1,128,512]{2,1,0:T(8,128)(2,1)} copy(bf16[1,128,512]{2,1,0:T(8,128)(2,1)S(1)} %bitcast.20) | data formatting | bytes 262144
  (6 shorter events, 0.1 us)
Async XLA Ops:
  2.5 18.8 %copy-start.4 = (bf16[1,128,512]{2,1,0:T(8,128)(2,1)S(1)}, bf16[1,128,512]{2,1,0:T(8,128)(2,1)}, u32[]{:S(2)}) copy-start(bf16[1,128,512]{2,1,0:T(8,128)(2,1)} %param.17) | copy-start | bytes 393220
  2.5 35.3 %copy-start.1 = (bf16[512,512]{1,0:T(8,128)(2,1)S(1)}, bf16[512,512]{1,0:T(8,128)(2,1)}, u32[]{:S(2)}) copy-start(bf16[512,512]{1,0:T(8,128)(2,1)} %refs_4_.3) | copy-start | bytes 1572868
  2.5 35.3 %copy-start.3 = (bf16[256,512]{1,0:T(8,128)(2,1)S(1)}, bf16[256,512]{1,0:T(8,128)(2,1)}, u32[]{:S(2)}) copy-start(bf16[256,512]{1,0:T(8,128)(2,1)} %refs_3_.1) | copy-start | bytes 786436
  2.5 35.6 %all-to-all-start = ((bf16[64,16,256]{2,1,0:T(8,128)(2,1)}), bf16[64,16,256]{2,1,0:T(8,128)(2,1)S(1)}, u32[]{:S(2)}, u32[]{:S(2)}) async-start(bf16[64,16,256]{2,1,0:T(8,128)(2,1)} %bitcast.5), calls=%async_computation | async-start | bytes 1048576 | tf_op jit(solution)/shard_map/all_to_all | solution.py:320
  14.8 23.1 %copy-start = (bf16[512,512]{1,0:T(8,128)(2,1)S(1)}, bf16[512,512]{1,0:T(8,128)(2,1)}, u32[]{:S(2)}) copy-start(bf16[512,512]{1,0:T(8,128)(2,1)} %refs_4_.2) | copy-start | bytes 1572868
  14.8 6.5 %collective-permute-start.1 = (bf16[4,16,512]{2,1,0:T(8,128)(2,1)}, bf16[4,16,512]{2,1,0:T(8,128)(2,1)S(1)}, u32[]{:S(2)}, u32[]{:S(2)}) collective-permute-start(bf16[4,16,512]{2,1,0:T(8,128)(2,1)} %param.2), channel_id=1, source_target_pairs={{0,1},{1,0},{2,3},{3,2},{4,5},{5,4},{6,7},{7,6},{8,9},{9,8},{10,11... | collective-permute-start | bytes 196616 | tf_op jit(solution)/shard_map/cond/branch_0_fun/ppermute | solution.py:212
  21.3 16.5 %copy-start.2 = (bf16[256,512]{1,0:T(8,128)(2,1)S(1)}, bf16[256,512]{1,0:T(8,128)(2,1)}, u32[]{:S(2)}) copy-start(bf16[256,512]{1,0:T(8,128)(2,1)} %refs_2_.1) | copy-start | bytes 786436
  21.4 11.7 %collective-permute-start.2 = (bf16[32,512]{1,0:T(8,128)(2,1)S(1)}, bf16[32,512]{1,0:T(8,128)(2,1)S(1)}, u32[]{:S(2)}, u32[]{:S(2)}) collective-permute-start(bf16[32,512]{1,0:T(8,128)(2,1)S(1)} %bitcast.21), channel_id=1, source_target_pairs={{0,6},{1,7},{2,4},{3,5},{4,2},{5,3},{6,0},{7,1},{8,14},{9,15},{10,... | collective-permute-start | bytes 98312 | tf_op jit(solution)/shard_map/ppermute | solution.py:212
  26.9 9.2 %collective-permute-start.3 = (bf16[32,512]{1,0:T(8,128)(2,1)S(1)}, bf16[32,512]{1,0:T(8,128)(2,1)S(1)}, u32[]{:S(2)}, u32[]{:S(2)}) collective-permute-start(bf16[32,512]{1,0:T(8,128)(2,1)S(1)} %bitcast.22), channel_id=1, source_target_pairs={{0,5},{1,4},{2,7},{3,6},{4,1},{5,0},{6,3},{7,2},{8,13},{9,12},{10,... | collective-permute-start | bytes 98312 | tf_op jit(solution)/shard_map/ppermute | solution.py:212
  30.9 6.9 %collective-permute-start.4 = (bf16[32,512]{1,0:T(8,128)(2,1)S(1)}, bf16[32,512]{1,0:T(8,128)(2,1)S(1)}, u32[]{:S(2)}, u32[]{:S(2)}) collective-permute-start(bf16[32,512]{1,0:T(8,128)(2,1)S(1)} %bitcast.23), channel_id=1, source_target_pairs={{0,2},{1,3},{2,0},{3,1},{4,6},{5,7},{6,4},{7,5},{8,10},{9,11},{10,... | collective-permute-start | bytes 98312 | tf_op jit(solution)/shard_map/ppermute | solution.py:212
